TPU v7x, 128 devices: a whole 4x4x4 slice. The times are simulated.
128 devices in a mesh: ctx: 32 (over y, x, core), dp: 4 (over z).
Axes of the slice: x: 4, y: 4, z: 4, core: 2. Of those that a mesh axis runs over, the one named last changes fastest.
Arguments:
- tokens: bfloat16 [4, 16384, 2048], P('dp', 'ctx'), may hold values from -6 to 6
- w_query: bfloat16 [2048, 1024], replicated, may hold values from -0.125 to 0.125
- w_key: bfloat16 [2048, 1024], replicated, may hold values from -0.125 to 0.125
- w_value: bfloat16 [2048, 1024], replicated, may hold values from -0.125 to 0.125
- cotangent: bfloat16 [4, 16384, 1024], P('dp', 'ctx'), may hold values from -6 to 6
Outputs:
- attn_out: bfloat16 [4, 16384, 1024], P('dp', 'ctx')
- input_grad: bfloat16 [4, 16384, 2048], P('dp', 'ctx')
- grad_query: float32 [2048, 1024], P(('ctx', 'dp'))
- grad_key: float32 [2048, 1024], P(('ctx', 'dp'))
- grad_value: float32 [2048, 1024], P(('ctx', 'dp'))
All inputs are finite; a program needn't handle non-finite values.
Results may differ from a plain program's by a relative error of at most 0.022.
Values may be sent and summed in bfloat16 or wider, within the bound.
No kernel may reach another device: no remote copies, remote signals or barrier semaphores. Data moves between devices by JAX's collectives and lax.ppermute only.
A program may use at most 192 MiB of HBM per device.

v0:
```python
import jax
import jax.numpy as jnp
from jax import lax
from jax.sharding import Mesh
from jax.sharding import PartitionSpec as P

HEADS = 8
DH = 128
CTX = ("ctx_0", "ctx_1", "ctx_2")
CTX_DP = ("ctx_0", "ctx_1", "ctx_2", "dp")


EPS = 1e-05


def nothing_yet(value, identity):
    return jnp.zeros_like(value) + jnp.asarray(identity, value.dtype)


def carried_in(value, axes, combine, identity, reverse):
    before = start = nothing_yet(value, identity)
    running = value
    for axis in reversed(axes):
        length, position = (lax.axis_size(axis), lax.axis_index(axis))
        pieces = lax.all_gather(running.astype(jnp.bfloat16), axis)
        inside, running = (start, start)
        for k in reversed(range(length)) if reverse else range(length):
            passed = k > position if reverse else k < position
            running = combine(running, pieces[k].astype(value.dtype))
            inside = jnp.where(passed, running, inside)
        before = combine(inside, before)
    return before


def split_up(value, dim, length):
    lengths = value.shape
    blocks = value.reshape(*lengths[:dim], length, lengths[dim] // length, *lengths[dim + 1 :])
    return jnp.moveaxis(blocks, dim, 0)


def sum_at_owner(value, axis, dim):
    length = lax.axis_size(axis)
    blocks = lax.all_to_all(split_up(value, dim, length), axis, 0, 0, tiled=True)
    return jnp.sum(blocks.astype(jnp.float32), axis=0)


def add_pair(earlier, later_part):
    return earlier + later_part


def per_device(tokens, w_query, w_key, w_value, cotangent):
    source = tokens[0]
    rows = source.shape[0]
    width = HEADS * DH
    query = (
        jnp.dot(source, w_query, preferred_element_type=jnp.float32)
        .astype(jnp.bfloat16)
        .reshape(rows, HEADS, DH)
    )
    key = (
        jnp.dot(source, w_key, preferred_element_type=jnp.float32)
        .astype(jnp.bfloat16)
        .reshape(rows, HEADS, DH)
    )
    value = (
        jnp.dot(source, w_value, preferred_element_type=jnp.float32)
        .astype(jnp.bfloat16)
        .reshape(rows, HEADS, DH)
    )
    zero_state = jnp.zeros((HEADS, DH, DH), jnp.float32)
    local_state = jnp.einsum("tha,thb->hab", key, value, preferred_element_type=jnp.float32).astype(
        jnp.bfloat16
    )
    prefix = carried_in(local_state.astype(jnp.float32), CTX, add_pair, zero_state, False)
    prefix = prefix.astype(jnp.bfloat16)
    index = jnp.arange(rows, dtype=jnp.int32)
    causal = (index[:, None] >= index[None, :]).astype(jnp.float32)
    scores = (
        jnp.einsum("tha,sha->hts", query, key, preferred_element_type=jnp.float32) * causal
    ).astype(jnp.bfloat16)
    mixed = jnp.einsum(
        "hts,shb->thb", scores, value, preferred_element_type=jnp.float32
    ) + jnp.einsum("tha,hab->thb", query, prefix, preferred_element_type=jnp.float32)
    inverse = lax.rsqrt(jnp.mean(mixed * mixed, axis=-1, keepdims=True) + EPS)
    normed = mixed * inverse
    attn_out = normed.astype(jnp.bfloat16).reshape(rows, width)
    upstream = cotangent[0].astype(jnp.float32).reshape(rows, HEADS, DH)
    grad_mixed = (
        (upstream - normed * jnp.mean(upstream * normed, axis=-1, keepdims=True)) * inverse
    ).astype(jnp.bfloat16)
    back_state = jnp.einsum(
        "tha,thb->hab", query, grad_mixed, preferred_element_type=jnp.float32
    ).astype(jnp.bfloat16)
    suffix = carried_in(back_state.astype(jnp.float32), CTX, add_pair, zero_state, True)
    suffix = suffix.astype(jnp.bfloat16)
    grad_scores = (
        jnp.einsum("thb,shb->hts", grad_mixed, value, preferred_element_type=jnp.float32) * causal
    ).astype(jnp.bfloat16)
    grad_q = jnp.einsum(
        "hts,sha->tha", grad_scores, key, preferred_element_type=jnp.float32
    ) + jnp.einsum("thb,hab->tha", grad_mixed, prefix, preferred_element_type=jnp.float32)
    grad_k = jnp.einsum(
        "hts,tha->sha", grad_scores, query, preferred_element_type=jnp.float32
    ) + jnp.einsum("shb,hab->sha", value, suffix, preferred_element_type=jnp.float32)
    grad_v = jnp.einsum(
        "hts,thb->shb", scores, grad_mixed, preferred_element_type=jnp.float32
    ) + jnp.einsum("sha,hab->shb", key, suffix, preferred_element_type=jnp.float32)
    grad_q = grad_q.astype(jnp.bfloat16).reshape(rows, width)
    grad_k = grad_k.astype(jnp.bfloat16).reshape(rows, width)
    grad_v = grad_v.astype(jnp.bfloat16).reshape(rows, width)
    input_grad = (
        jnp.dot(grad_q, w_query.T, preferred_element_type=jnp.float32)
        + jnp.dot(grad_k, w_key.T, preferred_element_type=jnp.float32)
        + jnp.dot(grad_v, w_value.T, preferred_element_type=jnp.float32)
    ).astype(jnp.bfloat16)
    combined = jnp.concatenate([grad_q, grad_k, grad_v], axis=1)
    ctx_count = lax.axis_size(CTX)
    dp_count = lax.axis_size("dp")
    partial_rows = lax.psum_scatter(
        jnp.dot(source.T, combined, preferred_element_type=jnp.float32).astype(jnp.bfloat16),
        CTX,
        scatter_dimension=0,
        tiled=True,
    )
    summed = sum_at_owner(partial_rows, "dp", 0)
    summed = summed * float(rows * ctx_count * dp_count) ** (-0.5)
    return (
        attn_out[None],
        input_grad[None],
        summed[:, :width],
        summed[:, width : 2 * width],
        summed[:, 2 * width :],
    )


def solution(mesh):
    finer = Mesh(mesh.devices.reshape(4, 4, 2, mesh.shape["dp"]), ("ctx_0", "ctx_1", "ctx_2", "dp"))
    return jax.shard_map(
        per_device,
        mesh=finer,
        in_specs=(P("dp", CTX, None), P(), P(), P(), P("dp", CTX, None)),
        out_specs=(
            P("dp", CTX, None),
            P("dp", CTX, None),
            P(CTX_DP, None),
            P(CTX_DP, None),
            P(CTX_DP, None),
        ),
        check_vma=False,
    )
```

profile of v0, /device:TPU:1, one launch (start us, length us, event | category | flops | bytes accessed | tf_op | source)
XLA Modules:
  0.0 302.6 jit_solution(11921921961809338224)
XLA Ops:
  8.8 4.7 %fusion.24 = bf16[64,8,8,128]{3,2,1,0:T(8,128)(2,1)S(1)} fusion(bf16[2048,1024]{1,0:T(8,128)(2,1)} %param.8, bf16[1,512,2048]{2,1,0:T(8,128)(2,1)S(1)} %copy-done), kind=kOutput, calls=%fused_computation.30 | convolution fusion | flops 2148007936 | bytes 7340032 | tf_op jit(solution)/shard_map/dot_general | solution.py:66
  13.5 2.4 fusion.21
  18.2 2.4 copy.52
  20.6 1.7 convolution_convert_fusion.1
  22.3 3.2 %all-gather = bf16[16,128,128]{2,1,0:T(8,128)(2,1)S(1)} all-gather(bf16[8,128,128]{2,1,0:T(8,128)(2,1)S(1)} %convolution_convert_fusion.1), channel_id=2, replica_groups=mesh['ctx_0'=4,'ctx_1'=4,'ctx_2'=2,'dp'=4] {'ctx_2'}, dimensions={0}, use_global_device_ids=true | all-gather | bytes 786432 | tf_op jit(solution)/shard_map/all_gather | solution.py:25
  27.2 25.3 %all-gather.7.cloned.1.call-done = bf16[4,8,128,128]{3,2,1,0:T(8,128)(2,1)} async-done(((bf16[1,8,128,128]{3,2,1,0:T(8,128)(2,1)}), bf16[4,8,128,128]{3,2,1,0:T(8,128)(2,1)}) %all-gather.7.cloned.1.call-update) | async-done | bytes 1048592 | tf_op jit(solution)/shard_map/all_gather | solution.py:25
  52.5 2.0 fusion.66
  54.8 5.5 %fusion.18 = bf16[512,1024]{1,0:T(8,128)(2,1)} fusion(bf16[2048,1024]{1,0:T(8,128)(2,1)} %param.6, bf16[1,512,2048]{2,1,0:T(8,128)(2,1)S(1)} %copy-done), kind=kOutput, calls=%fused_computation.28 | convolution fusion | flops 2148007936 | bytes 7340032 | tf_op jit(solution)/shard_map/dot_general | solution.py:56
  61.8 2.6 copy.56
  65.5 2.6 multiply_convert_fusion.1
  68.1 1.9 copy-done.2
  70.1 2.9 fusion.29
  73.0 6.1 %all-gather.9.cloned.1.call-done = bf16[4,8,128,128]{3,2,1,0:T(8,128)(2,1)} async-done(((bf16[1,8,128,128]{3,2,1,0:T(8,128)(2,1)}), bf16[4,8,128,128]{3,2,1,0:T(8,128)(2,1)}) %all-gather.9.cloned.1.call-update) | async-done | bytes 1048592 | tf_op jit(solution)/shard_map/all_gather | solution.py:25
  79.0 2.3 fusion.46
  81.4 2.1 fusion.6
  84.1 1.6 multiply_convert_fusion.2
  87.1 3.4 %all-gather.1 = bf16[16,128,128]{2,1,0:T(8,128)(2,1)S(1)} all-gather(bf16[8,128,128]{2,1,0:T(8,128)(2,1)S(1)} %convolution_convert_fusion), channel_id=3, replica_groups=mesh['ctx_0'=4,'ctx_1'=4,'ctx_2'=2,'dp'=4] {'ctx_2'}, dimensions={0}, use_global_device_ids=true | all-gather | bytes 786432 | tf_op jit(solution)/shard_map/all_gather | solution.py:25
  92.2 23.1 %all-gather.11.cloned.1.call-done = bf16[4,8,128,128]{3,2,1,0:T(8,128)(2,1)} async-done(((bf16[1,8,128,128]{3,2,1,0:T(8,128)(2,1)}), bf16[4,8,128,128]{3,2,1,0:T(8,128)(2,1)}) %all-gather.11.cloned.1.call-update) | async-done | bytes 1048592 | tf_op jit(solution)/shard_map/all_gather | solution.py:25
  115.3 2.0 fusion.65
  117.6 3.2 %multiply_convert_fusion = bf16[8,512,512]{2,1,0:T(8,128)(2,1)S(1)} fusion(f32[512,512]{1,0:T(8,128)} %copy-done.11, bf16[512,8,128]{0,2,1:T(8,128)(2,1)} %copy-done.4, bf16[64,8,8,128]{3,2,1,0:T(8,128)(2,1)} %copy-done.7), kind=kOutput, calls=%fused_computation.1 | convolution fusion | flops 541065216 | bytes 7340032 | tf_op jit(solution)/shard_map/thb,shb->hts/dot_general | solution.py:97
  123.9 2.1 fusion.79
  125.9 2.1 fusion.77
  128.0 13.8 %all-gather.13.cloned.1.call-done = bf16[4,8,128,128]{3,2,1,0:T(8,128)(2,1)} async-done(((bf16[1,8,128,128]{3,2,1,0:T(8,128)(2,1)}), bf16[4,8,128,128]{3,2,1,0:T(8,128)(2,1)}) %all-gather.13.cloned.1.call-update) | async-done | bytes 1048592 | tf_op jit(solution)/shard_map/all_gather | solution.py:25
  141.8 2.3 fusion.55
  144.2 2.5 add_convert_fusion.1
  148.2 13.2 %convert_bitcast_fusion = bf16[2048,3072]{0,1:T(8,128)(2,1)} fusion(bf16[512,1024]{0,1:T(8,128)(2,1)S(1)} %bitcast.129, bf16[512,1024]{0,1:T(8,128)(2,1)S(1)} %bitcast.131, bf16[512,1024]{0,1:T(8,128)(2,1)S(1)} %bitcast.127, bf16[1,512,2048]{2,1,0:T(8,128)(2,1)S(1)} %copy-done), kind=kOutput, calls=%fused_computation | convolution fusion | flops 6458179584 | bytes 17825792 | tf_op jit(solution)/shard_map/dot_general | solution.py:120
  161.5 16.7 %copy.74 = bf16[2048,3072]{1,0:T(8,128)(2,1)} copy(bf16[2048,3072]{0,1:T(8,128)(2,1)} %convert_bitcast_fusion) | data formatting | bytes 25165824
  180.7 6.7 %fusion.76 = f32[512,2048]{1,0:T(8,128)} fusion(bf16[512,1024]{0,1:T(8,128)(2,1)S(1)} %bitcast.128, bf16[2048,1024]{1,0:T(8,128)(2,1)} %param.6), kind=kOutput, calls=%fused_computation.103 | convolution fusion | flops 2147483648 | bytes 9437184 | tf_op jit(solution)/shard_map/dot_general | solution.py:112
  187.3 4.3 %fusion.78 = f32[512,2048]{1,0:T(8,128)} fusion(bf16[512,1024]{0,1:T(8,128)(2,1)S(1)} %bitcast.132, bf16[2048,1024]{1,0:T(8,128)(2,1)S(1)} %copy-done.24), kind=kOutput, calls=%fused_computation.105 | convolution fusion | flops 2147483648 | bytes 9437184 | tf_op jit(solution)/shard_map/dot_general | solution.py:113
  191.7 91.0 %reduce-scatter.4.cloned.1.call-done = bf16[64,3072]{1,0:T(8,128)(2,1)} async-done(((bf16[2048,3072]{1,0:T(8,128)(2,1)}), bf16[64,3072]{1,0:T(8,128)(2,1)}) %reduce-scatter.4.cloned.1.call-update) | async-done | bytes 393232 | tf_op jit(solution)/shard_map/reduce_scatter | solution.py:119
  282.6 4.1 %all-to-all-start = ((bf16[4,16,3072]{2,1,0:T(8,128)(2,1)}), bf16[4,16,3072]{2,1,0:T(8,128)(2,1)S(1)}, u32[]{:S(2)}, u32[]{:S(2)}) async-start(bf16[4,16,3072]{2,1,0:T(8,128)(2,1)} %bitcast.133), calls=%async_computation | async-start | bytes 786432 | tf_op jit(solution)/shard_map/all_to_all | solution.py:43
  286.8 8.5 %fusion.5 = bf16[1,512,2048]{2,1,0:T(8,128)(2,1)} fusion(bf16[512,1024]{0,1:T(8,128)(2,1)S(1)} %bitcast.130, bf16[2048,1024]{1,0:T(8,128)(2,1)} %param.8, f32[512,2048]{1,0:T(8,128)} %fusion.76, f32[512,2048]{1,0:T(8,128)} %fusion.78), kind=kOutput, calls=%fused_computation.9 | convolution fusion | flops 2150629376 | bytes 15728640 | tf_op jit(solution)/shard_map/dot_general | solution.py:114
  (76 shorter events, 20.1 us)
Async XLA Ops:
  7.2 1.6 copy-start
  7.2 45.3 %all-gather.7.cloned.1.call-start = ((), (), s32[]{:S(2)}) async-start(), calls=%async_computation.2 | async-start | bytes 1310720 | tf_op jit(solution)/shard_map/all_gather | solution.py:25
  8.8 4.7 %copy-start.23 = (bf16[2048,1024]{1,0:T(8,128)(2,1)S(1)}, bf16[2048,1024]{1,0:T(8,128)(2,1)}, u32[]{:S(2)}) copy-start(bf16[2048,1024]{1,0:T(8,128)(2,1)} %param.7) | copy-start | bytes 12582916
  13.4 7.2 %copy-start.7 = (bf16[64,8,8,128]{3,2,1,0:T(8,128)(2,1)}, bf16[64,8,8,128]{3,2,1,0:T(8,128)(2,1)S(1)}, u32[]{:S(2)}) copy-start(bf16[64,8,8,128]{3,2,1,0:T(8,128)(2,1)S(1)} %fusion.24) | copy-start | bytes 3145732
  15.8 1.1 copy-start.10
  25.5 0.8 copy-start.13
  27.1 51.9 %all-gather.9.cloned.1.call-start = ((), (), s32[]{:S(2)}) async-start(), calls=%async_computation.3 | async-start | bytes 1310720 | tf_op jit(solution)/shard_map/all_gather | solution.py:25
  54.6 60.8 %all-gather.11.cloned.1.call-start = ((), (), s32[]{:S(2)}) async-start(), calls=%async_computation.4 | async-start | bytes 1310720 | tf_op jit(solution)/shard_map/all_gather | solution.py:25
  64.4 5.7 %copy-start.8 = (bf16[64,8,8,128]{3,2,1,0:T(8,128)(2,1)S(1)}, bf16[64,8,8,128]{3,2,1,0:T(8,128)(2,1)}, u32[]{:S(2)}) copy-start(bf16[64,8,8,128]{3,2,1,0:T(8,128)(2,1)} %copy-done.7) | copy-start | bytes 3145732
  64.5 1.0 copy-start.11
  68.1 2.0 copy-start.2
  79.0 4.5 %copy-start.6 = (f32[1,512,1024]{1,2,0:T(8,128)S(1)}, f32[1,512,1024]{1,2,0:T(8,128)}, u32[]{:S(2)}) copy-start(f32[1,512,1024]{1,2,0:T(8,128)} %copy.56) | copy-start | bytes 6291460
  85.7 1.0 copy-start.4
  90.5 0.8 copy-start.14
  92.1 49.7 %all-gather.13.cloned.1.call-start = ((), (), s32[]{:S(2)}) async-start(), calls=%async_computation.5 | async-start | bytes 1310720 | tf_op jit(solution)/shard_map/all_gather | solution.py:25
  117.4 165.3 %reduce-scatter.4.cloned.1.call-start = ((), (), s32[]{:S(2)}) async-start(), calls=%async_computation.6 | async-start | bytes 12976128 | tf_op jit(solution)/shard_map/reduce_scatter | solution.py:119
  117.6 3.3 %copy-start.15 = (bf16[512,8,128]{0,2,1:T(8,128)(2,1)S(1)}, bf16[512,8,128]{0,2,1:T(8,128)(2,1)}, u32[]{:S(2)}) copy-start(bf16[512,8,128]{0,2,1:T(8,128)(2,1)} %copy.52) | copy-start | bytes 3145732
  120.9 1.5 copy-start.5
  120.9 3.0 copy-start.3
  128.0 18.7 %copy-start.9 = (bf16[64,8,8,128]{3,2,1,0:T(8,128)(2,1)S(1)}, bf16[64,8,8,128]{3,2,1,0:T(8,128)(2,1)}, u32[]{:S(2)}) copy-start(bf16[64,8,8,128]{3,2,1,0:T(8,128)(2,1)} %copy-done.7) | copy-start | bytes 3145732
  141.8 4.9 %copy-start.12 = (f32[8,128,512]{2,1,0:T(8,128)S(1)}, f32[8,128,512]{2,1,0:T(8,128)}, u32[]{:S(2)}) copy-start(f32[8,128,512]{2,1,0:T(8,128)} %fusion.77) | copy-start | bytes 6291460
  144.2 4.1 %copy-start.17 = (bf16[8,128,512]{2,1,0:T(8,128)(2,1)S(1)}, bf16[8,128,512]{2,1,0:T(8,128)(2,1)}, u32[]{:S(2)}) copy-start(bf16[8,128,512]{2,1,0:T(8,128)(2,1)} %add_convert_fusion.3) | copy-start | bytes 3145732
  146.7 1.0 copy-start.19
  147.2 1.0 copy-start.21
  178.1 1.2 copy-start.16
  178.1 2.5 copy-start.18
  180.7 6.7 %copy-start.22 = (bf16[8,128,512]{2,1,0:T(8,128)(2,1)S(1)}, bf16[8,128,512]{2,1,0:T(8,128)(2,1)}, u32[]{:S(2)}) copy-start(bf16[8,128,512]{2,1,0:T(8,128)(2,1)} %copy-done.21) | copy-start | bytes 3145732
  180.7 6.7 %copy-start.24 = (bf16[2048,1024]{1,0:T(8,128)(2,1)S(1)}, bf16[2048,1024]{1,0:T(8,128)(2,1)}, u32[]{:S(2)}) copy-start(bf16[2048,1024]{1,0:T(8,128)(2,1)} %param.7) | copy-start | bytes 12582916
  187.3 99.5 %copy-start.20 = (bf16[8,128,512]{2,1,0:T(8,128)(2,1)S(1)}, bf16[8,128,512]{2,1,0:T(8,128)(2,1)}, u32[]{:S(2)}) copy-start(bf16[8,128,512]{2,1,0:T(8,128)(2,1)} %copy-done.19) | copy-start | bytes 3145732
  282.6 12.7 %all-to-all-start = ((bf16[4,16,3072]{2,1,0:T(8,128)(2,1)}), bf16[4,16,3072]{2,1,0:T(8,128)(2,1)S(1)}, u32[]{:S(2)}, u32[]{:S(2)}) async-start(bf16[4,16,3072]{2,1,0:T(8,128)(2,1)} %bitcast.133), calls=%async_computation | async-start | bytes 786432 | tf_op jit(solution)/shard_map/all_to_all | solution.py:43
  286.8 9.3 %copy-start.1 = (bf16[1,512,2048]{2,1,0:T(8,128)(2,1)S(1)}, bf16[1,512,2048]{2,1,0:T(8,128)(2,1)}, u32[]{:S(2)}) copy-start(bf16[1,512,2048]{2,1,0:T(8,128)(2,1)} %param.5) | copy-start | bytes 6291460
Sparse Core Ops, SparseCore 0:
  27.3 25.1 all-gather.6
  54.7 24.3 all-gather.8
  92.3 23.0 all-gather.10
  117.5 24.3 all-gather.12
  178.3 104.3 reduce-scatter.3
where the time goes:
time: 304 us; the launch traced here: 303 us
  waiting for transfers between devices  159 us (52%)
  matrix products  68.3 us (22%)
  local copies, waits for them, and re-layouts  36.8 us (12%)
  between operations  14.1 us (5%)
  other arithmetic  12.6 us (4%)
  blocking collectives  6.6 us (2%)
  starting transfers between devices  4.75 us (2%)
    reduce_scatter x1, waiting for transfers between devices, per_device(): lax.psum_scatter(jnp.dot(source.T, combined, preferred_element_type=jnp.f...  91 us
    all_gather x4, waiting for transfers between devices, carried_in(): pieces = lax.all_gather(running.astype(jnp.bfloat16), axis)  68.3 us
    unnamed x53, local copies, waits for them, and re-layouts  29.7 us
    dot_general x1, matrix products, per_device(): jnp.dot(source.T, combined, preferred_element_type=jnp.float32)  13.2 us
    dot_general x1, matrix products, per_device(): jnp.dot(grad_v, w_value.T, preferred_element_type=jnp.float32)  8.53 us
    dot_general x1, matrix products, per_device(): jnp.dot(grad_q, w_query.T, preferred_element_type=jnp.float32)  6.66 us
    all_gather x2, blocking collectives, carried_in(): pieces = lax.all_gather(running.astype(jnp.bfloat16), axis)  6.6 us
  transfers between devices with their start and end apart: 6, of which 5 were waited for; matrix products, arithmetic and copies ran while one was open for 15% of the time, Pallas kernels for 0%

commit v1 on v0

v1 whole, which is shorter than its diff:
```python
import jax
import jax.numpy as jnp
from jax import lax
from jax.experimental import pallas as pl
from jax.experimental.pallas import tpu as pltpu
from jax.sharding import Mesh
from jax.sharding import PartitionSpec as P

DH = 128
TOK = 512
EPS = 1e-05
CTX = ("y", "x", "c")
CTX_DP = ("y", "x", "c", "z")
CHIPS = ("y", "x", "z")
BF = jnp.bfloat16
F32 = jnp.float32
MB = 1 << 20


def dot(a, b, ca=1, cb=0):
    return lax.dot_general(a, b, (((ca,), (cb,)), ((), ())), preferred_element_type=F32)


def causal(x):
    rows = lax.broadcasted_iota(jnp.int32, x.shape, 0)
    cols = lax.broadcasted_iota(jnp.int32, x.shape, 1)
    return jnp.where(rows >= cols, x, 0.0).astype(BF)


def head(h):
    return slice(h * DH, (h + 1) * DH)


def call(kernel, core, grid, ins, outs, flops, moved):
    return pl.pallas_call(
        kernel,
        out_shape=[jax.ShapeDtypeStruct(s, d) for s, d, _, _ in outs],
        grid_spec=pltpu.PrefetchScalarGridSpec(
            num_scalar_prefetch=1,
            grid=(grid,),
            in_specs=[pl.BlockSpec(b, m) for _, b, m in ins],
            out_specs=[pl.BlockSpec(b, m) for _, _, b, m in outs],
        ),
        compiler_params=pltpu.CompilerParams(
            dimension_semantics=("arbitrary",), vmem_limit_bytes=48 * MB
        ),
        cost_estimate=pl.CostEstimate(flops=flops, bytes_accessed=moved, transcendentals=0),
    )(core, *[a for a, _, _ in ins])


def whole(j, c):
    return (0, 0)


def tall(j, c):
    return (j, 0)


def wide(j, c):
    return (0, j)


def mine(j, c):
    return (0, c[0] * 2 + j)


def project_qkv(core, tok, wq, wk, wv):
    def kernel(c, t, a, b, d, q, k, v, s):
        x = t[...]
        q[...] = dot(x, a[...]).astype(BF)
        kk = dot(x, b[...]).astype(BF)
        vv = dot(x, d[...]).astype(BF)
        k[...] = kk
        v[...] = vv
        for h in range(2):
            s[head(h), :] = dot(kk[:, head(h)], vv[:, head(h)], 0, 0).astype(BF)

    w = (2048, 256)
    return call(
        kernel,
        core,
        2,
        [(tok, (TOK, 2048), whole), (wq, w, mine), (wk, w, mine), (wv, w, mine)],
        [((TOK, 512), BF, (TOK, 256), wide)] * 3 + [((512, DH), BF, (256, DH), tall)],
        3300000000,
        10 * MB,
    )


def project_kv(core, tok, wk, wv, state):
    def kernel(c, t, b, d, so, k, v, s, total):
        x = t[...]
        kk = dot(x, b[...]).astype(BF)
        vv = dot(x, d[...]).astype(BF)
        k[...] = kk
        v[...] = vv
        for h in range(2):
            st = dot(kk[:, head(h)], vv[:, head(h)], 0, 0).astype(BF)
            s[head(h), :] = st
            total[head(h), :] = (st.astype(F32) + so[head(h), :].astype(F32)).astype(BF)

    w = (2048, 256)
    return call(
        kernel,
        core,
        2,
        [(tok, (TOK, 2048), whole), (wk, w, mine), (wv, w, mine), (state, (256, DH), tall)],
        [((TOK, 512), BF, (TOK, 256), wide)] * 2 + [((512, DH), BF, (256, DH), tall)] * 2,
        2200000000,
        7 * MB,
    )


def within(core, tok_o, tok_p, wq, q_o, k_o, v_o, k_p, v_p):
    def kernel(c, to, tp, a, qo, ko, vo, kp, vp, qp, io, ip, tto, ttp):
        qq = dot(tp[...], a[...]).astype(BF)
        qp[...] = qq
        for q, k, v, out in ((qo[...], ko, vo, io), (qq, kp, vp, ip)):
            for h in range(2):
                scores = causal(dot(q[:, head(h)], k[:, head(h)], 1, 1))
                out[:, head(h)] = dot(scores, v[:, head(h)])
        cols = pl.ds(pl.multiple_of(pl.program_id(0) * 1024, 1024), 1024)
        tto[...] = to[:, cols].T
        ttp[...] = tp[:, cols].T

    b = (TOK, 256)
    return call(
        kernel,
        core,
        2,
        [(tok_o, (TOK, 2048), whole), (tok_p, (TOK, 2048), whole), (wq, (2048, 256), mine)]
        + [(t, b, wide) for t in (q_o, k_o, v_o, k_p, v_p)],
        [((TOK, 512), BF, b, wide)]
        + [((TOK, 512), F32, b, wide)] * 2
        + [((2048, TOK), BF, (1024, TOK), tall)] * 2,
        2200000000,
        15 * MB,
    )


def normed(core, i_o, i_p, q_o, q_p, p_o, p_p, cot, cot_p):
    def kernel(c, io, ip, qo, qp, po, pp, co, cp, ao, ap, go, gp, bo, bp, total):
        backs = []
        for i, q, p, ct, a, g, b in ((io, qo, po, co, ao, go, bo), (ip, qp, pp, cp, ap, gp, bp)):
            for h in range(2):
                qh = q[:, head(h)]
                mixed = i[:, head(h)] + dot(qh, p[head(h), :])
                inverse = lax.rsqrt(jnp.mean(mixed * mixed, axis=-1, keepdims=True) + EPS)
                n = mixed * inverse
                up = ct[:, head(h)].astype(F32)
                a[:, head(h)] = n.astype(BF)
                gm = ((up - n * jnp.mean(up * n, axis=-1, keepdims=True)) * inverse).astype(BF)
                g[:, head(h)] = gm
                back = dot(qh, gm, 0, 0).astype(BF)
                b[head(h), :] = back
                backs.append(back.astype(F32))
        for h in range(2):
            total[head(h), :] = (backs[h] + backs[2 + h]).astype(BF)

    b = (TOK, 256)
    s = (256, DH)
    return call(
        kernel,
        core,
        2,
        [(t, b, wide) for t in (i_o, i_p, q_o, q_p)]
        + [(p_o, s, tall), (p_p, s, tall), (cot, b, mine), (cot_p, b, wide)],
        [((TOK, 512), BF, b, wide)] * 4 + [((512, DH), BF, s, tall)] * 3,
        300000000,
        7 * MB,
    )


def grads_within(core, q_o, q_p, k_o, k_p, v_o, v_p, g_o, g_p, p_o, p_p):
    def kernel(c, qo, qp, ko, kp, vo, vp, go, gp, po, pp, dqo, dqp, dko, dkp, dvo, dvp):
        for q, k, v, g, p, dq, dk, dv in (
            (qo, ko, vo, go, po, dqo, dko, dvo),
            (qp, kp, vp, gp, pp, dqp, dkp, dvp),
        ):
            for h in range(2):
                qh, kh, vh, gh = (t[:, head(h)] for t in (q, k, v, g))
                gs = causal(dot(gh, vh, 1, 1))
                dq[:, head(h)] = (dot(gs, kh) + dot(gh, p[head(h), :], 1, 1)).astype(BF)
                dk[:, head(h)] = dot(gs, qh, 0, 0)
                scores = causal(dot(qh, kh, 1, 1))
                dv[:, head(h)] = dot(scores, gh, 0, 0)

    b = (TOK, 256)
    s = (256, DH)
    return call(
        kernel,
        core,
        2,
        [(t, b, wide) for t in (q_o, q_p, k_o, k_p, v_o, v_p, g_o, g_p)]
        + [(p_o, s, tall), (p_p, s, tall)],
        [((TOK, 512), BF, b, wide)] * 2 + [((TOK, 512), F32, b, wide)] * 4,
        2700000000,
        9 * MB,
    )


def grads_after(core, k_o, k_p, v_o, v_p, dk_o, dk_p, dv_o, dv_p, s_o, s_p):
    def kernel(c, ko, kp, vo, vp, ako, akp, avo, avp, so, sp, dko, dkp, dvo, dvp):
        for k, v, ak, av, s, dk, dv in (
            (ko, vo, ako, avo, so, dko, dvo),
            (kp, vp, akp, avp, sp, dkp, dvp),
        ):
            for h in range(2):
                dk[:, head(h)] = (ak[:, head(h)] + dot(v[:, head(h)], s[head(h), :], 1, 1)).astype(BF)
                dv[:, head(h)] = (av[:, head(h)] + dot(k[:, head(h)], s[head(h), :])).astype(BF)

    b = (TOK, 256)
    s = (256, DH)
    return call(
        kernel,
        core,
        2,
        [(t, b, wide) for t in (k_o, k_p, v_o, v_p, dk_o, dk_p, dv_o, dv_p)]
        + [(s_o, s, tall), (s_p, s, tall)],
        [((TOK, 512), BF, b, wide)] * 4,
        200000000,
        8 * MB,
    )


def weight_grad(core, tt_o, tt_p, grads):
    n = len(grads)

    def kernel(c, to, tp, *refs):
        out = refs[-1]
        for m in range(n):
            part = dot(to[...], refs[2 * m][...]) + dot(tp[...], refs[2 * m + 1][...])
            part = part.astype(BF)
            for x in range(4):
                for core_at in range(2):
                    for z in range(4):
                        row = x * 128 + core_at * 64 + z * 16
                        out[0, x, z, core_at * 16 : core_at * 16 + 16, m * 512 : m * 512 + 512] = part[
                            row : row + 16, :
                        ]

    flat = [t for pair in grads for t in pair]
    return call(
        kernel,
        core,
        4,
        [(tt_o, (512, TOK), tall), (tt_p, (512, TOK), tall)]
        + [(t, (TOK, 512), whole) for t in flat],
        [
            (
                (4, 4, 4, 32, n * 512),
                BF,
                (1, 4, 4, 32, n * 512),
                lambda j, c: (j, 0, 0, 0, 0),
            )
        ],
        2200000000 * n,
        (5 + 3 * n) * MB,
    )[0]


def input_part(core, grads, weights, received=None):
    def kernel(c, *refs):
        out = refs[-1]
        total = dot(refs[0][...], refs[3][...], 1, 1)
        total = total + dot(refs[1][...], refs[4][...], 1, 1)
        total = total + dot(refs[2][...], refs[5][...], 1, 1)
        if received is not None:
            total = total + refs[6][...].astype(F32)
        out[...] = total.astype(BF)

    ins = [(g, (TOK, 512), whole) for g in grads]
    ins += [(w, (512, 512), lambda j, c: (j, c[0])) for w in weights]
    if received is not None:
        ins.append((received, (TOK, 512), wide))
    return call(
        kernel, core, 4, ins, [((TOK, 2048), BF, (TOK, 512), wide)], 3300000000, 10 * MB
    )[0]


def shift(v, axis, d):
    n = lax.axis_size(axis)
    return lax.ppermute(v, axis, [(i, (i + d) % n) for i in range(n)])


def swap(v):
    return lax.ppermute(v, "c", [(0, 1), (1, 0)])


def scan_chips(total, reverse):
    before = None
    running = total
    for axis in ("x", "y"):
        at = lax.axis_index(axis)
        inside = jnp.zeros(total.shape, F32)
        row = running.astype(F32)
        for d in (1, 3, 2):
            piece = shift(running, axis, d).astype(F32)
            passed = at + (4 - d) < 4 if reverse else at >= d
            inside = inside + jnp.where(passed, piece, 0.0)
            row = row + piece
        before = inside if before is None else before + inside
        running = row.astype(BF)
    return before


def per_device(tokens, w_query, w_key, w_value, cotangent):
    c = lax.axis_index("c")
    core = c.astype(jnp.int32).reshape(1)
    tok_o = tokens[0]
    cot = cotangent[0]
    tok_p = swap(tok_o)
    cot_p = swap(lax.dynamic_slice(cot, (0, (1 - c) * 512), (TOK, 512)))

    q_o, k_o, v_o, state_o = project_qkv(core, tok_o, w_query, w_key, w_value)
    k_p, v_p, state_p, total = project_kv(core, tok_p, w_key, w_value, state_o)
    before = scan_chips(total, False)
    q_p, i_o, i_p, tt_o, tt_p = within(core, tok_o, tok_p, w_query, q_o, k_o, v_o, k_p, v_p)
    late = c == 1
    p_o = (before + jnp.where(late, state_p.astype(F32), 0.0)).astype(BF)
    p_p = (before + jnp.where(late, 0.0, state_o.astype(F32))).astype(BF)
    a_o, a_p, g_o, g_p, back_o, back_p, total = normed(
        core, i_o, i_p, q_o, q_p, p_o, p_p, cot, cot_p
    )
    after = scan_chips(total, True)
    a_r = swap(a_p)
    dq_o, dq_p, dk_o, dk_p, dv_o, dv_p = grads_within(
        core, q_o, q_p, k_o, k_p, v_o, v_p, g_o, g_p, p_o, p_p
    )
    part_q = weight_grad(core, tt_o, tt_p, [(dq_o, dq_p)])
    s_o = (after + jnp.where(late, 0.0, back_p.astype(F32))).astype(BF)
    s_p = (after + jnp.where(late, back_o.astype(F32), 0.0)).astype(BF)
    dk_o, dk_p, dv_o, dv_p = grads_after(
        core, k_o, k_p, v_o, v_p, dk_o, dk_p, dv_o, dv_p, s_o, s_p
    )
    part_kv = weight_grad(core, tt_o, tt_p, [(dk_o, dk_p), (dv_o, dv_p)])

    def to_owners(part):
        blocks = part.reshape(64, 32, part.shape[-1])
        blocks = lax.all_to_all(blocks, CHIPS, 0, 0, tiled=True)
        return jnp.sum(blocks.astype(F32), axis=0)

    sum_q = to_owners(part_q)
    sum_kv = to_owners(part_kv)
    weights = (w_query, w_key, w_value)
    ig_p = swap(input_part(core, (dq_p, dk_p, dv_p), weights))
    input_grad = input_part(core, (dq_o, dk_o, dv_o), weights, ig_p)
    attn_out = jnp.where(
        late, jnp.concatenate([a_r, a_o], axis=1), jnp.concatenate([a_o, a_r], axis=1)
    )
    summed = jnp.concatenate([sum_q, sum_kv], axis=1) * (65536.0**-0.5)
    own = lax.dynamic_slice(summed, (c * 16, 0), (16, 1536))
    other = lax.dynamic_slice(summed, ((1 - c) * 16, 0), (16, 1536))
    other = swap(other.astype(BF)).astype(F32)

    def joined(k):
        mine_k, other_k = own[:, k * 512 : k * 512 + 512], other[:, k * 512 : k * 512 + 512]
        return jnp.where(
            late,
            jnp.concatenate([other_k, mine_k], axis=1),
            jnp.concatenate([mine_k, other_k], axis=1),
        )

    return (attn_out[None], input_grad[None], joined(0), joined(1), joined(2))


def solution(mesh):
    finer = Mesh(mesh.devices.reshape(4, 4, 2, mesh.shape["dp"]), ("y", "x", "c", "z"))
    return jax.shard_map(
        per_device,
        mesh=finer,
        in_specs=(P("z", CTX, None), P(), P(), P(), P("z", CTX, None)),
        out_specs=(
            P("z", CTX, None),
            P("z", CTX, None),
            P(CTX_DP, None),
            P(CTX_DP, None),
            P(CTX_DP, None),
        ),
        check_vma=False,
    )
```

time: 304 us -> 193 us (0.63)
  waiting for transfers between devices: 159 us -> 60.6 us
  matrix products: 68.3 us -> 0 us
  Pallas kernels: 0 us -> 61.1 us
  starting transfers between devices: 4.75 us -> 44.6 us
  local copies, waits for them, and re-layouts: 36.8 us -> 12.1 us
  between operations: 14.1 us -> 0.88 us
  blocking collectives: 6.6 us -> 0 us
    reduce_scatter x1 -> x0, waiting for transfers between devices: 91 us -> none  [per_device(): lax.psum_scatter(jnp.dot(source.T, combined, preferred_element_type=jnp.f...]
    dot_general x19 -> x0, matrix products: 68.3 us -> none  [the longest x1 13.2 us: per_device(): jnp.dot(source.T, combined, preferred_element_type=jnp.float32)]
    all_gather x4 -> x0, waiting for transfers between devices: 68.3 us -> none  [carried_in(): pieces = lax.all_gather(running.astype(jnp.bfloat16), axis)]
    pallas_call x0 -> x10, Pallas kernels: none -> 61.1 us  [call(): pl.pallas_call(kernel, out_shape=[jax.ShapeDtypeStruct(s, d) for s, d, _,...]
    ppermute x0 -> x17, waiting for transfers between devices: none -> 38.8 us  [the longest x12 33.4 us: shift(): return lax.ppermute(v, axis, [(i, (i + d) % n) for i in range(n)])]
    ppermute x0 -> x17, starting transfers between devices: none -> 27.4 us  [the longest x12 17.1 us: shift(): return lax.ppermute(v, axis, [(i, (i + d) % n) for i in range(n)])]
    all_to_all x1 -> x2, waiting for transfers between devices: 0.01 us -> 21.8 us  [to_owners(): blocks = lax.all_to_all(blocks, CHIPS, 0, 0, tiled=True)]
    unnamed x53 -> x58, local copies, waits for them, and re-layouts: 29.7 us -> 10.3 us
  transfers between devices with their start and end apart: 6 -> 19, of which waited for: 5 -> 10; matrix products, arithmetic and copies ran while one was open for 15% -> 5% of each run, Pallas kernels for 0% -> 20%
where the time goes in v1:
time: 193 us; the launch traced here: 191 us
  Pallas kernels  61.1 us (32%)
  waiting for transfers between devices  60.6 us (31%)
  starting transfers between devices  44.6 us (23%)
  local copies, waits for them, and re-layouts  12.1 us (6%)
  other arithmetic  12 us (6%)
    pallas_call x10, Pallas kernels, call(): pl.pallas_call(kernel, out_shape=[jax.ShapeDtypeStruct(s, d) for s, d, _,...  61.1 us
    ppermute x12, waiting for transfers between devices, shift(): return lax.ppermute(v, axis, [(i, (i + d) % n) for i in range(n)])  33.4 us
    all_to_all x2, waiting for transfers between devices, to_owners(): blocks = lax.all_to_all(blocks, CHIPS, 0, 0, tiled=True)  21.8 us
    all_to_all x2, starting transfers between devices, to_owners(): blocks = lax.all_to_all(blocks, CHIPS, 0, 0, tiled=True)  17.2 us
    ppermute x12, starting transfers between devices, shift(): return lax.ppermute(v, axis, [(i, (i + d) % n) for i in range(n)])  17.1 us
    ppermute x5, starting transfers between devices, swap(): return lax.ppermute(v, 'c', [(0, 1), (1, 0)])  10.3 us
    unnamed x58, local copies, waits for them, and re-layouts  10.3 us
    ppermute x5, waiting for transfers between devices, swap(): return lax.ppermute(v, 'c', [(0, 1), (1, 0)])  5.4 us
  transfers between devices with their start and end apart: 19, of which 10 were waited for; matrix products, arithmetic and copies ran while one was open for 5% of the time, Pallas kernels for 20%

profile of v1, /device:TPU:1, one launch (start us, length us, event | category | flops | bytes accessed | tf_op | source)
XLA Modules:
  0.0 191.4 jit_solution(17508389490176930750)
XLA Ops:
  0.6 1.5 collective-permute-start
  2.1 1.6 copy-done
  3.7 6.3 %shard_map.92 = (bf16[512,512]{1,0:T(8,128)(2,1)S(1)}, bf16[512,512]{1,0:T(8,128)(2,1)S(1)}, bf16[512,512]{1,0:T(8,128)(2,1)S(1)}, bf16[512,128]{1,0:T(8,128)(2,1)S(1)}) custom-call(s32[1]{0:T(128)} %bitcast.c, bf16[512,2048]{1,0:T(8,128)(2,1)S(1)} %bitcast.12, bf16[2048,1024]{1,0:T(8,128)(2,1)} %refs_3_.3, bf16[2048,1024]{1,0:T(8,128)(2,1)} %refs_4_.3, ...), custom_call_target="tpu_custom_call" | custom-call | flops 3300000000 | bytes 10485760 | tf_op jit(solution)/shard_map/pallas_call | solution.py:35
  10.8 5.4 %shard_map.93 = (bf16[512,512]{1,0:T(8,128)(2,1)S(1)}, bf16[512,512]{1,0:T(8,128)(2,1)S(1)}, bf16[512,128]{1,0:T(8,128)(2,1)S(1)}, bf16[512,128]{1,0:T(8,128)(2,1)S(1)}) custom-call(s32[1]{0:T(128)} %bitcast.c, bf16[512,2048]{1,0:T(8,128)(2,1)S(1)} %collective-permute-done.t.tp, bf16[2048,1024]{1,0:T(8,128)(2,1)} %refs_4_.3, bf16[2048,1024]{1,0:T(8,128)(2,1)} %refs_5_.3, ...), custom_call_target="tpu_custom_call" | custom-call | flops 2200000000 | bytes 7340032 | tf_op jit(solution)/shard_map/pallas_call | solution.py:35
  17.8 2.8 %collective-permute-start.3 = (bf16[512,128]{1,0:T(8,128)(2,1)S(1)}, bf16[512,128]{1,0:T(8,128)(2,1)}, u32[]{:S(2)}, u32[]{:S(2)}) collective-permute-start(bf16[512,128]{1,0:T(8,128)(2,1)S(1)} %get-tuple-element.44), channel_id=1, source_target_pairs={{0,16},{8,24},{16,0},{24,8},{1,17},{9,25},{17,1},{25,9},{2,18},{10... | collective-permute-start | bytes 393224 | tf_op jit(solution)/shard_map/ppermute | solution.py:283
  22.1 1.9 dynamic-slice_bitcast_fusion
  24.8 2.7 %collective-permute-done.2 = bf16[512,128]{1,0:T(8,128)(2,1)} collective-permute-done((bf16[512,128]{1,0:T(8,128)(2,1)S(1)}, bf16[512,128]{1,0:T(8,128)(2,1)}, u32[]{:S(2)}, u32[]{:S(2)}) %collective-permute-start.2) | collective-permute-done | bytes 131104 | tf_op jit(solution)/shard_map/ppermute | solution.py:283
  28.6 3.0 %collective-permute-start.6 = (bf16[512,128]{1,0:T(8,128)(2,1)S(1)}, bf16[512,128]{1,0:T(8,128)(2,1)S(1)}, u32[]{:S(2)}, u32[]{:S(2)}) collective-permute-start(bf16[512,128]{1,0:T(8,128)(2,1)S(1)} %fusion.3), channel_id=1, source_target_pairs={{0,64},{32,96},{64,0},{96,32},{1,65},{33,97},{65,1},{97,33},{2,66}... | collective-permute-start | bytes 393224 | tf_op jit(solution)/shard_map/ppermute | solution.py:283
  33.1 8.0 %shard_map.94 = (bf16[512,512]{1,0:T(8,128)(2,1)S(1)}, f32[512,512]{1,0:T(8,128)S(1)}, f32[512,512]{1,0:T(8,128)S(1)}, bf16[2048,512]{1,0:T(8,128)(2,1)}, bf16[2048,512]{1,0:T(8,128)(2,1)}) custom-call(s32[1]{0:T(128)} %bitcast.c, bf16[512,2048]{1,0:T(8,128)(2,1)} %bitcast.11, bf16[512,2048]{1,0:T(8,128)(2,1)} %copy-done.1, bf16[2048,1024]{1,0:T(8,128)(2,1)} %refs_3_.3, ...), custom_call_target="tpu_custom_call" | custom-call | flops 2200000000 | bytes 15728640 | tf_op jit(solution)/shard_map/pallas_call | solution.py:35
  43.3 4.2 %shard_map.95 = (bf16[512,512]{1,0:T(8,128)(2,1)S(1)}, bf16[512,512]{1,0:T(8,128)(2,1)}, bf16[512,512]{1,0:T(8,128)(2,1)S(1)}, bf16[512,512]{1,0:T(8,128)(2,1)S(...) custom-call(s32[1]{0:T(128)} %bitcast.c, ...), custom_call_target="tpu_custom_call" | custom-call | flops 300000000 | bytes 7340032 | tf_op jit(solution)/shard_map/pallas_call | solution.py:35
  47.6 8.3 %shard_map.96 = (bf16[512,512]{1,0:T(8,128)(2,1)S(1)}, bf16[512,512]{1,0:T(8,128)(2,1)S(1)}, f32[512,512]{1,0:T(8,128)}, f32[512,512]{1,0:T(8,128)}, f32[512,512]{1,0:T(8,128)}, /*index=5*/f32[512,512]{1,0:T(8,128)}) custom-call(s32[1]{0:T(128)} %bitcast.c, bf16[512,512]{1,0:T(8,128)(2,1)S(1)} %get-tuple-element.35.qo, ...), custom_call_target="tpu_custom_call" | custom-call | flops 2700000000 | bytes 9437184 | tf_op jit(solution)/shard_map/pallas_call | solution.py:35
  55.9 5.6 %shard_map.100 = bf16[4,4,4,32,512]{4,3,2,1,0:T(8,128)(2,1)} custom-call(s32[1]{0:T(128)} %bitcast.c, bf16[2048,512]{1,0:T(8,128)(2,1)S(1)} %copy-done.24, bf16[2048,512]{1,0:T(8,128)(2,1)} %get-tuple-element.64.tp, bf16[512,512]{1,0:T(8,128)(2,1)S(1)} %get-tuple-element.50.refs_0_, bf16[512,512]{1,0:T(8,128)(2,1)S(1)} %get-tuple-element.60.refs_0_.refs_1_), custom_call_target="tpu_custom_call" | custom-call | flops 2200000000 | bytes 8388608 | tf_op jit(solution)/shard_map/pallas_call | solution.py:35
  61.6 10.7 %all-to-all-start = ((bf16[64,32,512]{2,1,0:T(8,128)(2,1)}), bf16[64,32,512]{2,1,0:T(8,128)(2,1)}, u32[]{:S(2)}, u32[]{:S(2)}) async-start(bf16[64,32,512]{2,1,0:T(8,128)(2,1)} %bitcast.7), calls=%async_computation | async-start | bytes 4194304 | tf_op jit(solution)/shard_map/all_to_all | solution.py:340
  72.3 2.5 %collective-permute-start.11 = (bf16[512,128]{1,0:T(8,128)(2,1)S(1)}, bf16[512,128]{1,0:T(8,128)(2,1)S(1)}, u32[]{:S(2)}, u32[]{:S(2)}) collective-permute-start(bf16[512,128]{1,0:T(8,128)(2,1)S(1)} %get-tuple-element.55), channel_id=1, source_target_pairs={{0,16},{8,24},{16,0},{24,8},{1,17},{9,25},{17,1},{25,9},{2,18},{10... | collective-permute-start | bytes 393224 | tf_op jit(solution)/shard_map/ppermute | solution.py:283
  76.3 22.5 %collective-permute-done.11 = bf16[512,128]{1,0:T(8,128)(2,1)S(1)} collective-permute-done((bf16[512,128]{1,0:T(8,128)(2,1)S(1)}, bf16[512,128]{1,0:T(8,128)(2,1)S(1)}, u32[]{:S(2)}, u32[]{:S(2)}) %collective-permute-start.11) | collective-permute-done | bytes 131104 | tf_op jit(solution)/shard_map/ppermute | solution.py:283
  98.8 1.3 collective-permute-done.10
  101.7 2.9 %collective-permute-start.14 = (bf16[512,128]{1,0:T(8,128)(2,1)}, bf16[512,128]{1,0:T(8,128)(2,1)S(1)}, u32[]{:S(2)}, u32[]{:S(2)}) collective-permute-start(bf16[512,128]{1,0:T(8,128)(2,1)} %fusion.7), channel_id=1, source_target_pairs={{0,64},{32,96},{64,0},{96,32},{1,65},{33,97},{65,1},{97,33},{2,66}... | collective-permute-start | bytes 393224 | tf_op jit(solution)/shard_map/ppermute | solution.py:283
  107.3 1.9 collective-permute-done.13
  109.2 3.0 %collective-permute-done.12 = bf16[512,128]{1,0:T(8,128)(2,1)} collective-permute-done((bf16[512,128]{1,0:T(8,128)(2,1)}, bf16[512,128]{1,0:T(8,128)(2,1)}, u32[]{:S(2)}, u32[]{:S(2)}) %collective-permute-start.12) | collective-permute-done | bytes 131104 | tf_op jit(solution)/shard_map/ppermute | solution.py:283
  112.1 1.3 add_convert_fusion
  113.6 2.7 %shard_map.97 = (bf16[512,512]{1,0:T(8,128)(2,1)S(1)}, bf16[512,512]{1,0:T(8,128)(2,1)S(1)}, bf16[512,512]{1,0:T(8,128)(2,1)S(1)}, bf16[512,512]{1,0:T(8,128)(2,1)S(1)}) custom-call(s32[1]{0:T(128)} %bitcast.c, bf16[512,512]{1,0:T(8,128)(2,1)S(1)} %get-tuple-element.36.ko, bf16[512,512]{1,0:T(8,128)(2,1)S(1)} %copy-done.5, bf16[512,512]{1,0:T(8,128)(2,1)S(1)} %copy-done.3, ...), custom_call_target="tpu_custom_call" | custom-call | flops 200000000 | bytes 8388608 | tf_op jit(solution)/shard_map/pallas_call | solution.py:35
  116.3 7.3 %shard_map.101 = bf16[4,4,4,32,1024]{4,3,2,1,0:T(8,128)(2,1)} custom-call(s32[1]{0:T(128)} %bitcast.c, bf16[2048,512]{1,0:T(8,128)(2,1)S(1)} %copy-done.25, bf16[2048,512]{1,0:T(8,128)(2,1)} %get-tuple-element.64.tp, bf16[512,512]{1,0:T(8,128)(2,1)S(1)} %get-tuple-element.58.refs_1_.refs_0_, bf16[512,512]{1,0:T(8,128)(2,1)S(1)} %get-tuple-element.61.refs_1_, ...), custom_call_target="tpu_custom_call" | custom-call | flops 4400000000 | bytes 11534336 | tf_op jit(solution)/shard_map/pallas_call | solution.py:35
  126.7 6.5 %all-to-all-start.1 = ((bf16[64,32,1024]{2,1,0:T(8,128)(2,1)}), bf16[64,32,1024]{2,1,0:T(8,128)(2,1)}, u32[]{:S(2)}, u32[]{:S(2)}) async-start(bf16[64,32,1024]{2,1,0:T(8,128)(2,1)} %bitcast.14), calls=%async_computation.1 | async-start | bytes 8388608 | tf_op jit(solution)/shard_map/all_to_all | solution.py:340
  135.4 6.0 %shard_map.98 = bf16[512,2048]{1,0:T(8,128)(2,1)S(1)} custom-call(s32[1]{0:T(128)} %bitcast.c, bf16[512,512]{1,0:T(8,128)(2,1)S(1)} %copy-done.13, bf16[512,512]{1,0:T(8,128)(2,1)S(1)} %copy-done.15, bf16[512,512]{1,0:T(8,128)(2,1)S(1)} %copy-done.17, bf16[2048,1024]{1,0:T(8,128)(2,1)} %refs_3_.3, bf16[2048,1024]{1,0:T(8,128)(2,1)} %refs_4_.3, ...), custom_call_target="tpu_custom_call" | custom-call | flops 3300000000 | bytes 10485760 | tf_op jit(solution)/shard_map/pallas_call | solution.py:35
  141.4 3.4 %collective-permute-start.15 = (bf16[512,2048]{1,0:T(8,128)(2,1)S(1)}, bf16[512,2048]{1,0:T(8,128)(2,1)}, u32[]{:S(2)}, u32[]{:S(2)}) collective-permute-start(bf16[512,2048]{1,0:T(8,128)(2,1)S(1)} %shard_map.98), channel_id=1, source_target_pairs={{0,4},{4,0},{1,5},{5,1},{2,6},{6,2},{3,7},{7,3},{8,12},{12,8},{9,1... | collective-permute-start | bytes 6291464 | tf_op jit(solution)/shard_map/ppermute | solution.py:287
  144.8 4.5 %collective-permute-done.8 = bf16[512,512]{1,0:T(8,128)(2,1)S(1)} collective-permute-done((bf16[512,512]{1,0:T(8,128)(2,1)}, bf16[512,512]{1,0:T(8,128)(2,1)S(1)}, u32[]{:S(2)}, u32[]{:S(2)}) %collective-permute-start.8) | collective-permute-done | bytes 524320 | tf_op jit(solution)/shard_map/ppermute | solution.py:287
  149.4 1.3 maximum_select_fusion
  150.6 1.9 %convert_reduce_fusion.1 = f32[32,512]{1,0:T(8,128)S(1)} fusion(bf16[64,32,512]{2,1,0:T(8,128)(2,1)} %all-to-all-done), kind=kLoop, calls=%fused_computation.1 | loop fusion | flops 2080768 | bytes 2162688 | tf_op jit(solution)/shard_map/reduce_sum | solution.py:341
  152.6 7.3 %shard_map.99 = bf16[512,2048]{1,0:T(8,128)(2,1)} custom-call(s32[1]{0:T(128)} %bitcast.c, bf16[512,512]{1,0:T(8,128)(2,1)S(1)} %copy-done.19, bf16[512,512]{1,0:T(8,128)(2,1)S(1)} %copy-done.21, bf16[512,512]{1,0:T(8,128)(2,1)S(1)} %copy-done.23, bf16[2048,1024]{1,0:T(8,128)(2,1)} %refs_3_.3, bf16[2048,1024]{1,0:T(8,128)(2,1)} %refs_4_.3, ...), custom_call_target="tpu_custom_call" | custom-call | flops 3300000000 | bytes 10485760 | tf_op jit(solution)/shard_map/pallas_call | solution.py:35
  159.9 21.8 %all-to-all-done.1 = bf16[64,32,1024]{2,1,0:T(8,128)(2,1)} async-done(((bf16[64,32,1024]{2,1,0:T(8,128)(2,1)}), bf16[64,32,1024]{2,1,0:T(8,128)(2,1)}, u32[]{:S(2)}, u32[]{:S(2)}) %all-to-all-start.1) | async-done | bytes 4194336 | tf_op jit(solution)/shard_map/all_to_all | solution.py:340
  181.7 3.0 %convert_reduce_fusion = f32[32,1024]{1,0:T(8,128)S(1)} fusion(bf16[64,32,1024]{2,1,0:T(8,128)(2,1)} %all-to-all-done.1), kind=kLoop, calls=%fused_computation | loop fusion | flops 4161536 | bytes 4325376 | tf_op jit(solution)/shard_map/reduce_sum | solution.py:341
  184.8 4.5 %collective-permute-start.16 = (bf16[16,1536]{1,0:T(8,128)(2,1)S(1)}, bf16[16,1536]{1,0:T(8,128)(2,1)S(1)}, u32[]{:S(2)}, u32[]{:S(2)}) collective-permute-start(bf16[16,1536]{1,0:T(8,128)(2,1)S(1)} %dynamic-slice_convert_fusion), channel_id=1, source_target_pairs={{0,4},{4,0},{1,5},{5,1},{2,6},{6,2},{3,7},{7,3},{8,12},{12,8},{9,1... | collective-permute-start | bytes 147464 | tf_op jit(solution)/shard_map/ppermute | solution.py:287
  (90 shorter events, 22.9 us)
Async XLA Ops:
  0.6 10.2 %collective-permute-start = (bf16[512,2048]{1,0:T(8,128)(2,1)}, bf16[512,2048]{1,0:T(8,128)(2,1)S(1)}, u32[]{:S(2)}, u32[]{:S(2)}) collective-permute-start(bf16[512,2048]{1,0:T(8,128)(2,1)} %bitcast.10), channel_id=1, source_target_pairs={{0,4},{4,0},{1,5},{5,1},{2,6},{6,2},{3,7},{7,3},{8,12},{12,8},{9,1... | collective-permute-start | bytes 6291464 | tf_op jit(solution)/shard_map/ppermute | solution.py:287
  10.8 5.4 %copy-start.1 = (bf16[512,2048]{1,0:T(8,128)(2,1)}, bf16[512,2048]{1,0:T(8,128)(2,1)S(1)}, u32[]{:S(2)}) copy-start(bf16[512,2048]{1,0:T(8,128)(2,1)S(1)} %collective-permute-done.t.tp) | copy-start | bytes 6291460
  17.8 15.2 %copy-start.3 = (bf16[512,512]{1,0:T(8,128)(2,1)S(1)}, bf16[512,512]{1,0:T(8,128)(2,1)}, u32[]{:S(2)}) copy-start(bf16[512,512]{1,0:T(8,128)(2,1)} %copy-done.2) | copy-start | bytes 1572868
  17.8 15.2 %copy-start.5 = (bf16[512,512]{1,0:T(8,128)(2,1)S(1)}, bf16[512,512]{1,0:T(8,128)(2,1)}, u32[]{:S(2)}) copy-start(bf16[512,512]{1,0:T(8,128)(2,1)} %copy-done.4) | copy-start | bytes 1572868
  17.8 15.2 %copy-start.7 = (bf16[512,512]{1,0:T(8,128)(2,1)S(1)}, bf16[512,512]{1,0:T(8,128)(2,1)}, u32[]{:S(2)}) copy-start(bf16[512,512]{1,0:T(8,128)(2,1)} %copy-done.6) | copy-start | bytes 1572868
  17.8 7.0 %collective-permute-start.3 = (bf16[512,128]{1,0:T(8,128)(2,1)S(1)}, bf16[512,128]{1,0:T(8,128)(2,1)}, u32[]{:S(2)}, u32[]{:S(2)}) collective-permute-start(bf16[512,128]{1,0:T(8,128)(2,1)S(1)} %get-tuple-element.44), channel_id=1, source_target_pairs={{0,16},{8,24},{16,0},{24,8},{1,17},{9,25},{17,1},{25,9},{2,18},{10... | collective-permute-start | bytes 393224 | tf_op jit(solution)/shard_map/ppermute | solution.py:283
  20.6 6.9 %collective-permute-start.2 = (bf16[512,128]{1,0:T(8,128)(2,1)S(1)}, bf16[512,128]{1,0:T(8,128)(2,1)}, u32[]{:S(2)}, u32[]{:S(2)}) collective-permute-start(bf16[512,128]{1,0:T(8,128)(2,1)S(1)} %get-tuple-element.44), channel_id=1, source_target_pairs={{0,24},{8,0},{16,8},{24,16},{1,25},{9,1},{17,9},{25,17},{2,26},{10... | collective-permute-start | bytes 393224 | tf_op jit(solution)/shard_map/ppermute | solution.py:283
  21.5 6.0 %collective-permute-start.1 = (bf16[512,128]{1,0:T(8,128)(2,1)S(1)}, bf16[512,128]{1,0:T(8,128)(2,1)}, u32[]{:S(2)}, u32[]{:S(2)}) collective-permute-start(bf16[512,128]{1,0:T(8,128)(2,1)S(1)} %get-tuple-element.44), channel_id=1, source_target_pairs={{0,8},{8,16},{16,24},{24,0},{1,9},{9,17},{17,25},{25,1},{2,10},{10... | collective-permute-start | bytes 393224 | tf_op jit(solution)/shard_map/ppermute | solution.py:283
  24.0 19.4 %collective-permute-start.7 = (bf16[512,512]{1,0:T(8,128)(2,1)}, bf16[512,512]{1,0:T(8,128)(2,1)S(1)}, u32[]{:S(2)}, u32[]{:S(2)}) collective-permute-start(bf16[512,512]{1,0:T(8,128)(2,1)} %dynamic-slice_bitcast_fusion), channel_id=1, source_target_pairs={{0,4},{4,0},{1,5},{5,1},{2,6},{6,2},{3,7},{7,3},{8,12},{12,8},{9,1... | collective-permute-start | bytes 1572872 | tf_op jit(solution)/shard_map/ppermute | solution.py:287
  28.6 13.4 %collective-permute-start.6 = (bf16[512,128]{1,0:T(8,128)(2,1)S(1)}, bf16[512,128]{1,0:T(8,128)(2,1)S(1)}, u32[]{:S(2)}, u32[]{:S(2)}) collective-permute-start(bf16[512,128]{1,0:T(8,128)(2,1)S(1)} %fusion.3), channel_id=1, source_target_pairs={{0,64},{32,96},{64,0},{96,32},{1,65},{33,97},{65,1},{97,33},{2,66}... | collective-permute-start | bytes 393224 | tf_op jit(solution)/shard_map/ppermute | solution.py:283
  31.6 10.5 %collective-permute-start.5 = (bf16[512,128]{1,0:T(8,128)(2,1)S(1)}, bf16[512,128]{1,0:T(8,128)(2,1)S(1)}, u32[]{:S(2)}, u32[]{:S(2)}) collective-permute-start(bf16[512,128]{1,0:T(8,128)(2,1)S(1)} %fusion.3), channel_id=1, source_target_pairs={{0,96},{32,0},{64,32},{96,64},{1,97},{33,1},{65,33},{97,65},{2,98}... | collective-permute-start | bytes 393224 | tf_op jit(solution)/shard_map/ppermute | solution.py:283
  32.4 9.7 %collective-permute-start.4 = (bf16[512,128]{1,0:T(8,128)(2,1)S(1)}, bf16[512,128]{1,0:T(8,128)(2,1)S(1)}, u32[]{:S(2)}, u32[]{:S(2)}) collective-permute-start(bf16[512,128]{1,0:T(8,128)(2,1)S(1)} %fusion.3), channel_id=1, source_target_pairs={{0,32},{32,64},{64,96},{96,0},{1,33},{33,65},{65,97},{97,1},{2,34}... | collective-permute-start | bytes 393224 | tf_op jit(solution)/shard_map/ppermute | solution.py:283
  47.6 8.3 %copy-start.10 = (bf16[512,512]{1,0:T(8,128)(2,1)}, bf16[512,512]{1,0:T(8,128)(2,1)S(1)}, u32[]{:S(2)}) copy-start(bf16[512,512]{1,0:T(8,128)(2,1)S(1)} %get-tuple-element.47) | copy-start | bytes 1572868
  47.6 8.4 %copy-start.24 = (bf16[2048,512]{1,0:T(8,128)(2,1)S(1)}, bf16[2048,512]{1,0:T(8,128)(2,1)}, u32[]{:S(2)}) copy-start(bf16[2048,512]{1,0:T(8,128)(2,1)} %get-tuple-element.63.to) | copy-start | bytes 6291460
  55.9 5.7 %copy-start.12 = (bf16[512,512]{1,0:T(8,128)(2,1)}, bf16[512,512]{1,0:T(8,128)(2,1)S(1)}, u32[]{:S(2)}) copy-start(bf16[512,512]{1,0:T(8,128)(2,1)S(1)} %get-tuple-element.60.refs_0_.refs_1_) | copy-start | bytes 1572868
  55.9 5.7 %copy-start.18 = (bf16[512,512]{1,0:T(8,128)(2,1)}, bf16[512,512]{1,0:T(8,128)(2,1)S(1)}, u32[]{:S(2)}) copy-start(bf16[512,512]{1,0:T(8,128)(2,1)S(1)} %get-tuple-element.50.refs_0_) | copy-start | bytes 1572868
  61.6 65.1 %all-to-all-start = ((bf16[64,32,512]{2,1,0:T(8,128)(2,1)}), bf16[64,32,512]{2,1,0:T(8,128)(2,1)}, u32[]{:S(2)}, u32[]{:S(2)}) async-start(bf16[64,32,512]{2,1,0:T(8,128)(2,1)} %bitcast.7), calls=%async_computation | async-start | bytes 4194304 | tf_op jit(solution)/shard_map/all_to_all | solution.py:340
  72.3 41.3 %copy-start.9 = (f32[512,512]{1,0:T(8,128)S(1)}, f32[512,512]{1,0:T(8,128)}, u32[]{:S(2)}) copy-start(f32[512,512]{1,0:T(8,128)} %get-tuple-element.51.ako) | copy-start | bytes 3145732
  72.3 26.5 %collective-permute-start.11 = (bf16[512,128]{1,0:T(8,128)(2,1)S(1)}, bf16[512,128]{1,0:T(8,128)(2,1)S(1)}, u32[]{:S(2)}, u32[]{:S(2)}) collective-permute-start(bf16[512,128]{1,0:T(8,128)(2,1)S(1)} %get-tuple-element.55), channel_id=1, source_target_pairs={{0,16},{8,24},{16,0},{24,8},{1,17},{9,25},{17,1},{25,9},{2,18},{10... | collective-permute-start | bytes 393224 | tf_op jit(solution)/shard_map/ppermute | solution.py:283
  74.8 25.3 %collective-permute-start.10 = (bf16[512,128]{1,0:T(8,128)(2,1)S(1)}, bf16[512,128]{1,0:T(8,128)(2,1)S(1)}, u32[]{:S(2)}, u32[]{:S(2)}) collective-permute-start(bf16[512,128]{1,0:T(8,128)(2,1)S(1)} %get-tuple-element.55), channel_id=1, source_target_pairs={{0,24},{8,0},{16,8},{24,16},{1,25},{9,1},{17,9},{25,17},{2,26},{10... | collective-permute-start | bytes 393224 | tf_op jit(solution)/shard_map/ppermute | solution.py:283
  75.7 25.3 %collective-permute-start.9 = (bf16[512,128]{1,0:T(8,128)(2,1)S(1)}, bf16[512,128]{1,0:T(8,128)(2,1)S(1)}, u32[]{:S(2)}, u32[]{:S(2)}) collective-permute-start(bf16[512,128]{1,0:T(8,128)(2,1)S(1)} %get-tuple-element.55), channel_id=1, source_target_pairs={{0,8},{8,16},{16,24},{24,0},{1,9},{9,17},{17,25},{25,1},{2,10},{10... | collective-permute-start | bytes 393224 | tf_op jit(solution)/shard_map/ppermute | solution.py:283
  100.1 4.6 %copy-start.27 = (bf16[512,128]{1,0:T(8,128)(2,1)}, bf16[512,128]{1,0:T(8,128)(2,1)S(1)}, u32[]{:S(2)}) copy-start(bf16[512,128]{1,0:T(8,128)(2,1)S(1)} %collective-permute-done.10) | copy-start | bytes 393220
  101.0 4.5 %copy-start.28 = (bf16[512,128]{1,0:T(8,128)(2,1)}, bf16[512,128]{1,0:T(8,128)(2,1)S(1)}, u32[]{:S(2)}) copy-start(bf16[512,128]{1,0:T(8,128)(2,1)S(1)} %collective-permute-done.9) | copy-start | bytes 393220
  101.7 5.5 %collective-permute-start.14 = (bf16[512,128]{1,0:T(8,128)(2,1)}, bf16[512,128]{1,0:T(8,128)(2,1)S(1)}, u32[]{:S(2)}, u32[]{:S(2)}) collective-permute-start(bf16[512,128]{1,0:T(8,128)(2,1)} %fusion.7), channel_id=1, source_target_pairs={{0,64},{32,96},{64,0},{96,32},{1,65},{33,97},{65,1},{97,33},{2,66}... | collective-permute-start | bytes 393224 | tf_op jit(solution)/shard_map/ppermute | solution.py:283
  104.7 4.5 %collective-permute-start.13 = (bf16[512,128]{1,0:T(8,128)(2,1)}, bf16[512,128]{1,0:T(8,128)(2,1)}, u32[]{:S(2)}, u32[]{:S(2)}) collective-permute-start(bf16[512,128]{1,0:T(8,128)(2,1)} %fusion.7), channel_id=1, source_target_pairs={{0,96},{32,0},{64,32},{96,64},{1,97},{33,1},{65,33},{97,65},{2,98}... | collective-permute-start | bytes 393224 | tf_op jit(solution)/shard_map/ppermute | solution.py:283
  105.5 6.7 %collective-permute-start.12 = (bf16[512,128]{1,0:T(8,128)(2,1)}, bf16[512,128]{1,0:T(8,128)(2,1)}, u32[]{:S(2)}, u32[]{:S(2)}) collective-permute-start(bf16[512,128]{1,0:T(8,128)(2,1)} %fusion.7), channel_id=1, source_target_pairs={{0,32},{32,64},{64,96},{96,0},{1,33},{33,65},{65,97},{97,1},{2,34}... | collective-permute-start | bytes 393224 | tf_op jit(solution)/shard_map/ppermute | solution.py:283
  126.7 6.5 %copy-start.13 = (bf16[512,512]{1,0:T(8,128)(2,1)S(1)}, bf16[512,512]{1,0:T(8,128)(2,1)}, u32[]{:S(2)}) copy-start(bf16[512,512]{1,0:T(8,128)(2,1)} %copy-done.12) | copy-start | bytes 1572868
  126.7 55.0 %all-to-all-start.1 = ((bf16[64,32,1024]{2,1,0:T(8,128)(2,1)}), bf16[64,32,1024]{2,1,0:T(8,128)(2,1)}, u32[]{:S(2)}, u32[]{:S(2)}) async-start(bf16[64,32,1024]{2,1,0:T(8,128)(2,1)} %bitcast.14), calls=%async_computation.1 | async-start | bytes 8388608 | tf_op jit(solution)/shard_map/all_to_all | solution.py:340
  135.4 14.0 %copy-start.11 = (bf16[512,512]{1,0:T(8,128)(2,1)S(1)}, bf16[512,512]{1,0:T(8,128)(2,1)}, u32[]{:S(2)}) copy-start(bf16[512,512]{1,0:T(8,128)(2,1)} %copy-done.10) | copy-start | bytes 1572868
  141.4 11.2 %collective-permute-start.15 = (bf16[512,2048]{1,0:T(8,128)(2,1)S(1)}, bf16[512,2048]{1,0:T(8,128)(2,1)}, u32[]{:S(2)}, u32[]{:S(2)}) collective-permute-start(bf16[512,2048]{1,0:T(8,128)(2,1)S(1)} %shard_map.98), channel_id=1, source_target_pairs={{0,4},{4,0},{1,5},{5,1},{2,6},{6,2},{3,7},{7,3},{8,12},{12,8},{9,1... | collective-permute-start | bytes 6291464 | tf_op jit(solution)/shard_map/ppermute | solution.py:287
  144.7 4.6 %collective-permute-start.8 = (bf16[512,512]{1,0:T(8,128)(2,1)}, bf16[512,512]{1,0:T(8,128)(2,1)S(1)}, u32[]{:S(2)}, u32[]{:S(2)}) collective-permute-start(bf16[512,512]{1,0:T(8,128)(2,1)} %get-tuple-element.46), channel_id=1, source_target_pairs={{0,4},{4,0},{1,5},{5,1},{2,6},{6,2},{3,7},{7,3},{8,12},{12,8},{9,1... | collective-permute-start | bytes 1572872 | tf_op jit(solution)/shard_map/ppermute | solution.py:287
  184.8 5.3 %collective-permute-start.16 = (bf16[16,1536]{1,0:T(8,128)(2,1)S(1)}, bf16[16,1536]{1,0:T(8,128)(2,1)S(1)}, u32[]{:S(2)}, u32[]{:S(2)}) collective-permute-start(bf16[16,1536]{1,0:T(8,128)(2,1)S(1)} %dynamic-slice_convert_fusion), channel_id=1, source_target_pairs={{0,4},{4,0},{1,5},{5,1},{2,6},{6,2},{3,7},{7,3},{8,12},{12,8},{9,1... | collective-permute-start | bytes 147464 | tf_op jit(solution)/shard_map/ppermute | solution.py:287
  (16 other events, 25.5 us)

commit v2 on v1

v2 whole, which is shorter than its diff:
```python
import jax
import jax.numpy as jnp
from jax import lax
from jax.experimental import pallas as pl
from jax.experimental.pallas import tpu as pltpu
from jax.sharding import Mesh
from jax.sharding import PartitionSpec as P

DH = 128
TOK = 512
EPS = 1e-05
CTX = ("y", "x", "c")
CTX_DP = ("y", "x", "c", "z")
BF = jnp.bfloat16
F32 = jnp.float32
MB = 1 << 20


def dot(a, b, ca=1, cb=0):
    return lax.dot_general(a, b, (((ca,), (cb,)), ((), ())), preferred_element_type=F32)


def causal(x, first=0):
    rows = lax.broadcasted_iota(jnp.int32, x.shape, 0) + first
    cols = lax.broadcasted_iota(jnp.int32, x.shape, 1)
    return jnp.where(rows >= cols, x, 0.0).astype(BF)


def head(h):
    return slice(h * DH, (h + 1) * DH)


def call(kernel, core, grid, ins, outs, flops, moved):
    return pl.pallas_call(
        kernel,
        out_shape=[jax.ShapeDtypeStruct(s, d) for s, d, _, _ in outs],
        grid_spec=pltpu.PrefetchScalarGridSpec(
            num_scalar_prefetch=1,
            grid=(grid,),
            in_specs=[pl.BlockSpec(b, m) for _, b, m in ins],
            out_specs=[pl.BlockSpec(b, m) for _, _, b, m in outs],
        ),
        compiler_params=pltpu.CompilerParams(
            dimension_semantics=("arbitrary",), vmem_limit_bytes=30 * MB
        ),
        cost_estimate=pl.CostEstimate(flops=flops, bytes_accessed=moved, transcendentals=0),
    )(core, *[a for a, _, _ in ins])


def whole(j, c):
    return (0, 0)


def tall(j, c):
    return (j, 0)


def wide(j, c):
    return (0, j)


def mine(j, c):
    return (0, c[0] * 2 + j)


def project_qkv(core, tok, wq, wk, wv):
    def kernel(c, t, a, b, d, q, k, v, s):
        x = t[...]
        q[...] = dot(x, a[...]).astype(BF)
        kk = dot(x, b[...]).astype(BF)
        vv = dot(x, d[...]).astype(BF)
        k[...] = kk
        v[...] = vv
        for h in range(2):
            s[head(h), :] = dot(kk[:, head(h)], vv[:, head(h)], 0, 0).astype(BF)

    w = (2048, 256)
    return call(
        kernel,
        core,
        2,
        [(tok, (TOK, 2048), whole), (wq, w, mine), (wk, w, mine), (wv, w, mine)],
        [((TOK, 512), BF, (TOK, 256), wide)] * 3 + [((512, DH), BF, (256, DH), tall)],
        3300000000,
        10 * MB,
    )


def project_kv(core, tok, wk, wv, state):
    def kernel(c, t, b, d, so, k, v, s, total):
        x = t[...]
        kk = dot(x, b[...]).astype(BF)
        vv = dot(x, d[...]).astype(BF)
        k[...] = kk
        v[...] = vv
        for h in range(2):
            st = dot(kk[:, head(h)], vv[:, head(h)], 0, 0).astype(BF)
            s[head(h), :] = st
            total[head(h), :] = (st.astype(F32) + so[head(h), :].astype(F32)).astype(BF)

    w = (2048, 256)
    return call(
        kernel,
        core,
        2,
        [(tok, (TOK, 2048), whole), (wk, w, mine), (wv, w, mine), (state, (256, DH), tall)],
        [((TOK, 512), BF, (TOK, 256), wide)] * 2 + [((512, DH), BF, (256, DH), tall)] * 2,
        2200000000,
        7 * MB,
    )


def half_rows(x, r):
    return x[r * 256 : r * 256 + 256]


def attend(q, k, r):
    return causal(dot(half_rows(q, r), k[: r * 256 + 256], 1, 1), r * 256)


def rows_down(s0, s1, x):
    first = dot(s0, x[:256], 0, 0) + dot(s1[:, :256], x[256:], 0, 0)
    return first, dot(s1[:, 256:], x[256:], 0, 0)


def within(core, tok_p, wq, q_o, k_o, v_o, k_p, v_p):
    def kernel(c, tp, a, qo, ko, vo, kp, vp, qp, out):
        qq = dot(tp[...], a[...]).astype(BF)
        qp[...] = qq
        for n, (q, k, v) in enumerate(((qo[...], ko, vo), (qq, kp, vp))):
            for h in range(2):
                qh, kh, vh = q[:, head(h)], k[:, head(h)], v[:, head(h)]
                out[n * TOK : n * TOK + 256, head(h)] = dot(attend(qh, kh, 0), vh[:256])
                out[n * TOK + 256 : n * TOK + 512, head(h)] = dot(attend(qh, kh, 1), vh)

    b = (TOK, 256)
    return call(
        kernel,
        core,
        2,
        [(tok_p, (TOK, 2048), whole), (wq, (2048, 256), mine)]
        + [(t, b, wide) for t in (q_o, k_o, v_o, k_p, v_p)],
        [((TOK, 512), BF, b, wide), ((2 * TOK, 512), F32, (2 * TOK, 256), wide)],
        2200000000,
        10 * MB,
    )


def turned(core, tok_o, tok_p):
    def kernel(c, to, tp, out):
        out[:, :TOK] = to[...].T
        out[:, TOK:] = tp[...].T

    return call(
        kernel,
        core,
        4,
        [(tok_o, (TOK, 512), wide), (tok_p, (TOK, 512), wide)],
        [((2048, 2 * TOK), BF, (512, 2 * TOK), tall)],
        1000000,
        8 * MB,
    )[0]


def normed(core, intra, q_o, q_p, p_o, p_p, cot, cot_p):
    def kernel(c, it, qo, qp, po, pp, co, cp, ao, ap, g, bo, bp, total):
        backs = []
        for n, (q, p, ct, a, b) in enumerate(((qo, po, co, ao, bo), (qp, pp, cp, ap, bp))):
            rows = slice(n * TOK, n * TOK + TOK)
            for h in range(2):
                qh = q[:, head(h)]
                mixed = it[rows, head(h)] + dot(qh, p[head(h), :])
                inverse = lax.rsqrt(jnp.mean(mixed * mixed, axis=-1, keepdims=True) + EPS)
                nm = mixed * inverse
                up = ct[:, head(h)].astype(F32)
                a[:, head(h)] = nm.astype(BF)
                gm = ((up - nm * jnp.mean(up * nm, axis=-1, keepdims=True)) * inverse).astype(BF)
                g[rows, head(h)] = gm
                back = dot(qh, gm, 0, 0).astype(BF)
                b[head(h), :] = back
                backs.append(back.astype(F32))
        for h in range(2):
            total[head(h), :] = (backs[h] + backs[2 + h]).astype(BF)

    b = (TOK, 256)
    s = (256, DH)
    return call(
        kernel,
        core,
        2,
        [(intra, (2 * TOK, 256), wide)]
        + [(t, b, wide) for t in (q_o, q_p)]
        + [(p_o, s, tall), (p_p, s, tall), (cot, b, mine), (cot_p, b, wide)],
        [((TOK, 512), BF, b, wide)] * 2
        + [((2 * TOK, 512), BF, (2 * TOK, 256), wide)]
        + [((512, DH), BF, s, tall)] * 3,
        300000000,
        7 * MB,
    )


def grad_q_of(core, k_o, k_p, v_o, v_p, g, p_o, p_p):
    def kernel(c, ko, kp, vo, vp, gr, po, pp, dq):
        for n, (k, v, p) in enumerate(((ko, vo, po), (kp, vp, pp))):
            for h in range(2):
                kh, vh = k[:, head(h)], v[:, head(h)]
                gh = gr[n * TOK : n * TOK + TOK, head(h)]
                past = dot(gh, p[head(h), :], 1, 1)
                for r in range(2):
                    at = n * TOK + r * 256
                    now = dot(attend(gh, vh, r), kh[: r * 256 + 256])
                    dq[at : at + 256, head(h)] = (now + half_rows(past, r)).astype(BF)

    b = (TOK, 256)
    s = (256, DH)
    return call(
        kernel,
        core,
        2,
        [(t, b, wide) for t in (k_o, k_p, v_o, v_p)]
        + [(g, (2 * TOK, 256), wide), (p_o, s, tall), (p_p, s, tall)],
        [((2 * TOK, 512), BF, (2 * TOK, 256), wide)],
        1200000000,
        4 * MB,
    )[0]


def grads_within(core, q_o, q_p, k_o, k_p, v_o, v_p, g):
    def kernel(c, qo, qp, ko, kp, vo, vp, gr, dk, dv):
        for n, (q, k, v) in enumerate(((qo, ko, vo), (qp, kp, vp))):
            for h in range(2):
                qh, kh, vh = q[:, head(h)], k[:, head(h)], v[:, head(h)]
                gh = gr[n * TOK : n * TOK + TOK, head(h)]
                for left, right, x, out in ((gh, vh, qh, dk), (qh, kh, gh, dv)):
                    first, second = rows_down(attend(left, right, 0), attend(left, right, 1), x)
                    out[n * TOK : n * TOK + 256, head(h)] = first
                    out[n * TOK + 256 : n * TOK + 512, head(h)] = second

    b = (TOK, 256)
    return call(
        kernel,
        core,
        2,
        [(t, b, wide) for t in (q_o, q_p, k_o, k_p, v_o, v_p)] + [(g, (2 * TOK, 256), wide)],
        [((2 * TOK, 512), F32, (2 * TOK, 256), wide)] * 2,
        2000000000,
        9 * MB,
    )


def grads_after(core, k_o, k_p, v_o, v_p, dk, dv, s_o, s_p):
    def kernel(c, ko, kp, vo, vp, ak, av, so, sp, ok, ov):
        for n, (k, v, s) in enumerate(((ko, vo, so), (kp, vp, sp))):
            rows = slice(n * TOK, n * TOK + TOK)
            for h in range(2):
                sh = s[head(h), :]
                ok[rows, head(h)] = (ak[rows, head(h)] + dot(v[:, head(h)], sh, 1, 1)).astype(BF)
                ov[rows, head(h)] = (av[rows, head(h)] + dot(k[:, head(h)], sh)).astype(BF)

    b = (TOK, 256)
    s = (256, DH)
    both = (2 * TOK, 256)
    return call(
        kernel,
        core,
        2,
        [(t, b, wide) for t in (k_o, k_p, v_o, v_p)]
        + [(dk, both, wide), (dv, both, wide), (s_o, s, tall), (s_p, s, tall)],
        [((2 * TOK, 512), BF, both, wide)] * 2,
        200000000,
        8 * MB,
    )


def weight_grad(core, tt, grad, first, steps):
    n = len(steps)
    step_at = lambda j: sum(jnp.where(j == i, s, 0) for i, s in enumerate(steps))
    if first == "x":
        block = (4, 1, 8, 16, 2 * TOK)
        at = lambda j, c: (0, (c[2] + step_at(j)) % 4, 0, 0, 0)
    elif first == "y":
        block = (1, 4, 8, 16, 2 * TOK)
        at = lambda j, c: ((c[1] + step_at(j)) % 4, 0, 0, 0, 0)
    else:
        block = (2, 4, 8, 16, 2 * TOK)
        at = lambda j, c: (j, 0, 0, 0, 0)

    def kernel(c, t, g, out):
        rows = block[0] * block[1] * 128
        part = dot(t[...].reshape(rows, 2 * TOK), g[...]).astype(BF)
        j = pl.program_id(0)
        for a in range(block[0]):
            for b in range(block[1]):
                for core_at in range(2):
                    for z in range(4):
                        row = ((a * block[1] + b) * 2 + core_at) * 64 + z * 16
                        piece = part[row : row + 16, :]
                        here = slice(core_at * 16, core_at * 16 + 16)
                        dz = (z - c[3] + 4) % 4
                        if first == "x":
                            out[0, (a - c[1] + 4) % 4, dz, here, :] = piece
                        elif first == "y":
                            out[0, (b - c[2] + 4) % 4, dz, here, :] = piece
                        else:
                            dy = (j * 2 + a - c[1] + 4) % 4
                            out[dz, (b - c[2] + 4) % 4, dy, here, :] = piece

    if first == "z":
        grid, shape, out_block, out_at = 2, (4, 4, 4, 32, 512), (4, 4, 4, 32, 512), None
        out_at = lambda j, c: (0, 0, 0, 0, 0)
    else:
        grid, shape, out_block = n, (n, 4, 4, 32, 512), (1, 4, 4, 32, 512)
        out_at = lambda j, c: (j, 0, 0, 0, 0)
    return call(
        kernel,
        core,
        grid,
        [
            (tt.reshape(4, 4, 8, 16, 2 * TOK), block, at),
            (grad, (2 * TOK, 512), whole),
        ],
        [(shape, BF, out_block, out_at)],
        550000000 * n,
        (1 + 2 * n) * MB,
    )[0]


def input_part(core, slot, grads, weights, received=None):
    def kernel(c, *refs):
        out = refs[-1]
        total = dot(refs[0][...], refs[3][...], 1, 1)
        total = total + dot(refs[1][...], refs[4][...], 1, 1)
        total = total + dot(refs[2][...], refs[5][...], 1, 1)
        if received is not None:
            total = total + refs[6][...].astype(F32)
        out[...] = total.astype(BF)

    ins = [(g, (TOK, 512), lambda j, c: (slot, 0)) for g in grads]
    ins += [(w, (512, 512), lambda j, c: (j, c[0])) for w in weights]
    if received is not None:
        ins.append((received, (TOK, 512), wide))
    return call(
        kernel, core, 4, ins, [((TOK, 2048), BF, (TOK, 512), wide)], 3300000000, 10 * MB
    )[0]


def shift(v, axis, d):
    n = lax.axis_size(axis)
    return lax.ppermute(v, axis, [(i, (i + d) % n) for i in range(n)])


def swap(v):
    return lax.ppermute(v, "c", [(0, 1), (1, 0)])


def scan_axis(running, axis, reverse):
    at = lax.axis_index(axis)
    inside = jnp.zeros(running.shape, F32)
    row = running.astype(F32)
    for d in (1, 3, 2):
        piece = shift(running, axis, d).astype(F32)
        passed = at + (4 - d) < 4 if reverse else at >= d
        inside = inside + jnp.where(passed, piece, 0.0)
        row = row + piece
    return inside, row.astype(BF)


def together(*values):
    return lax.optimization_barrier(values)


def f32_sum(*parts):
    total = parts[0].astype(F32)
    for p in parts[1:]:
        total = total + p.astype(F32)
    return total.astype(BF)


def ring_out(far, axis):
    return shift(far[:2], axis, 1), shift(far[2:], axis, 3)


def ring_near(up, down, came, axis):
    from_left, from_right = came
    up = jnp.concatenate([f32_sum(up[:2], from_left), up[2:]], axis=0)
    down = jnp.concatenate([down[:2], f32_sum(down[2:], from_right)], axis=0)
    return shift(up, axis, 1), shift(down, axis, 3)


def spread(blocks, axis):
    return f32_sum(blocks[0], *[shift(blocks[d], axis, d) for d in (1, 3, 2)])


def per_device(tokens, w_query, w_key, w_value, cotangent):
    c = lax.axis_index("c")
    core = jnp.stack([lax.axis_index(a) for a in ("c", "y", "x", "z")]).astype(jnp.int32)
    tok_o = tokens[0]
    cot = cotangent[0]
    tok_p = swap(tok_o)
    late = c == 1
    cot_p = swap(jnp.where(late, cot[:, :512], cot[:, 512:]))

    q_o, k_o, v_o, state_o = project_qkv(core, tok_o, w_query, w_key, w_value)
    k_p, v_p, state_p, total = project_kv(core, tok_p, w_key, w_value, state_o)
    before, row = scan_axis(total, "x", False)
    q_p, intra = within(core, tok_p, w_query, q_o, k_o, v_o, k_p, v_p)
    row, intra, q_p = together(row, intra, q_p)
    rows_before, _ = scan_axis(row, "y", False)
    tt = turned(core, tok_o, tok_p)
    rows_before, tt = together(rows_before, tt)
    before = before + rows_before
    p_o = (before + jnp.where(late, state_p.astype(F32), 0.0)).astype(BF)
    p_p = (before + jnp.where(late, 0.0, state_o.astype(F32))).astype(BF)
    a_o, a_p, g, back_o, back_p, total = normed(core, intra, q_o, q_p, p_o, p_p, cot, cot_p)
    after, row = scan_axis(total, "x", True)
    dq = grad_q_of(core, k_o, k_p, v_o, v_p, g, p_o, p_p)
    part_q = weight_grad(core, tt, dq, "z", (0, 1, 2, 3))
    row, part_q = together(row, part_q)
    rows_after, _ = scan_axis(row, "y", True)
    came_q = ring_out(part_q[2], "z")
    dk, dv = grads_within(core, q_o, q_p, k_o, k_p, v_o, v_p, g)
    rows_after, dk, dv = together(rows_after, dk, dv)
    after = after + rows_after
    s_o = (after + jnp.where(late, 0.0, back_p.astype(F32))).astype(BF)
    s_p = (after + jnp.where(late, back_o.astype(F32), 0.0)).astype(BF)
    dk, dv = grads_after(core, k_o, k_p, v_o, v_p, dk, dv, s_o, s_p)
    far_k = weight_grad(core, tt, dk, "x", (2,))[0]
    far_v = weight_grad(core, tt, dv, "y", (2,))[0]
    far_k, far_v, *came_q = together(far_k, far_v, *came_q)
    near_q = ring_near(part_q[1], part_q[3], came_q, "z")
    came_k = ring_out(far_k, "x")
    came_v = ring_out(far_v, "y")
    near_k = weight_grad(core, tt, dk, "x", (1, 3, 0))
    near_v = weight_grad(core, tt, dv, "y", (1, 3, 0))
    near_k, near_v, *came = together(near_k, near_v, *came_k, *came_v)
    last_k = ring_near(near_k[0], near_k[1], came[:2], "x")
    last_v = ring_near(near_v[0], near_v[1], came[2:], "y")
    weights = (w_query, w_key, w_value)
    ig_p = input_part(core, 1, (dq, dk, dv), weights)
    ig_p, *last = together(ig_p, *last_k, *last_v, *near_q)
    sum_k = f32_sum(near_k[2], *last[:2])
    sum_v = f32_sum(near_v[2], *last[2:4])
    sum_q = f32_sum(part_q[0], *last[4:])
    sum_k = spread(sum_k, "y")
    sum_vq = spread(jnp.stack([sum_v, sum_q], axis=1), "x")
    ig_r = swap(ig_p)
    a_r = swap(a_p)
    input_grad = input_part(core, 0, (dq, dk, dv), weights, ig_r)
    input_grad, sum_k, sum_vq = together(input_grad, sum_k, sum_vq)
    sum_kv = spread(jnp.concatenate([sum_k, sum_vq[0]], axis=-1), "z")
    sum_q = spread(sum_vq[1], "y")
    attn_out = jnp.where(
        late, jnp.concatenate([a_r, a_o], axis=1), jnp.concatenate([a_o, a_r], axis=1)
    )
    summed = jnp.concatenate([sum_q, sum_kv], axis=1)
    own = jnp.where(late, summed[16:], summed[:16])
    other = swap(jnp.where(late, summed[:16], summed[16:]))
    scale = 65536.0**-0.5
    left = jnp.where(late, other, own).astype(F32) * scale
    right = jnp.where(late, own, other).astype(F32) * scale

    def joined(k):
        cols = slice(k * 512, k * 512 + 512)
        return jnp.concatenate([left[:, cols], right[:, cols]], axis=1)

    return (attn_out[None], input_grad[None], joined(0), joined(1), joined(2))


def solution(mesh):
    finer = Mesh(mesh.devices.reshape(4, 4, 2, mesh.shape["dp"]), ("y", "x", "c", "z"))
    return jax.shard_map(
        per_device,
        mesh=finer,
        in_specs=(P("z", CTX, None), P(), P(), P(), P("z", CTX, None)),
        out_specs=(
            P("z", CTX, None),
            P("z", CTX, None),
            P(CTX_DP, None),
            P(CTX_DP, None),
            P(CTX_DP, None),
        ),
        check_vma=False,
    )
```

time: 193 us -> 164 us (0.85)
  waiting for transfers between devices: 60.6 us -> 26.2 us
  starting transfers between devices: 44.6 us -> 58.3 us
  other arithmetic: 12 us -> 8.65 us
  Pallas kernels: 61.1 us -> 57.9 us
    ppermute x12 -> x36, starting transfers between devices: 17.1 us -> 45 us  [shift(): return lax.ppermute(v, axis, [(i, (i + d) % n) for i in range(n)])]
    all_to_all x2 -> x0, waiting for transfers between devices: 21.8 us -> none  [to_owners(): blocks = lax.all_to_all(blocks, CHIPS, 0, 0, tiled=True)]
    all_to_all x2 -> x0, starting transfers between devices: 17.2 us -> none  [to_owners(): blocks = lax.all_to_all(blocks, CHIPS, 0, 0, tiled=True)]
    ppermute x12 -> x36, waiting for transfers between devices: 33.4 us -> 26.2 us  [shift(): return lax.ppermute(v, axis, [(i, (i + d) % n) for i in range(n)])]
    ppermute x5, waiting for transfers between devices: 5.4 us -> 0.01 us  [swap(): return lax.ppermute(v, 'c', [(0, 1), (1, 0)])]
    reduce_sum x2 -> x0, other arithmetic: 4.94 us -> none  [to_owners(): return jnp.sum(blocks.astype(F32), axis=0)]
    pallas_call x10 -> x15, Pallas kernels: 61.1 us -> 57.9 us  [call(): pl.pallas_call(kernel, out_shape=[jax.ShapeDtypeStruct(s, d) for s, d, _,...]
    ppermute x5, starting transfers between devices: 10.3 us -> 13.3 us  [swap(): return lax.ppermute(v, 'c', [(0, 1), (1, 0)])]
  transfers between devices with their start and end apart: 19 -> 41, of which waited for: 10 -> 10; matrix products, arithmetic and copies ran while one was open for 5% -> 4% of each run, Pallas kernels for 20% -> 30%
where the time goes in v2:
time: 164 us; the launch traced here: 163 us
  starting transfers between devices  58.3 us (36%)
  Pallas kernels  57.9 us (35%)
  waiting for transfers between devices  26.2 us (16%)
  local copies, waits for them, and re-layouts  11 us (7%)
  other arithmetic  8.65 us (5%)
    pallas_call x15, Pallas kernels, call(): pl.pallas_call(kernel, out_shape=[jax.ShapeDtypeStruct(s, d) for s, d, _,...  57.9 us
    ppermute x36, starting transfers between devices, shift(): return lax.ppermute(v, axis, [(i, (i + d) % n) for i in range(n)])  45 us
    ppermute x36, waiting for transfers between devices, shift(): return lax.ppermute(v, axis, [(i, (i + d) % n) for i in range(n)])  26.2 us
    ppermute x5, starting transfers between devices, swap(): return lax.ppermute(v, 'c', [(0, 1), (1, 0)])  13.3 us
    unnamed x54, local copies, waits for them, and re-layouts  10.7 us
  transfers between devices with their start and end apart: 41, of which 10 were waited for; matrix products, arithmetic and copies ran while one was open for 4% of the time, Pallas kernels for 30%

profile of v2, /device:TPU:1, one launch (start us, length us, event | category | flops | bytes accessed | tf_op | source)
XLA Modules:
  0.0 163.5 jit_solution(4521097536246193495)
XLA Ops:
  2.2 2.2 %copy-done = bf16[2048,1024]{1,0:T(8,128)(2,1)S(1)} copy-done((bf16[2048,1024]{1,0:T(8,128)(2,1)S(1)}, bf16[2048,1024]{1,0:T(8,128)(2,1)}, u32[]{:S(2)}) %copy-start) | copy-done | bytes 4194328
  4.4 2.2 %copy-done.3 = bf16[2048,1024]{1,0:T(8,128)(2,1)S(1)} copy-done((bf16[2048,1024]{1,0:T(8,128)(2,1)S(1)}, bf16[2048,1024]{1,0:T(8,128)(2,1)}, u32[]{:S(2)}) %copy-start.3) | copy-done | bytes 4194328
  6.6 2.2 %copy-done.6 = bf16[2048,1024]{1,0:T(8,128)(2,1)S(1)} copy-done((bf16[2048,1024]{1,0:T(8,128)(2,1)S(1)}, bf16[2048,1024]{1,0:T(8,128)(2,1)}, u32[]{:S(2)}) %copy-start.6) | copy-done | bytes 4194328
  10.4 5.8 %shard_map.92 = (bf16[512,512]{1,0:T(8,128)(2,1)S(1)}, bf16[512,512]{1,0:T(8,128)(2,1)S(1)}, bf16[512,512]{1,0:T(8,128)(2,1)S(1)}, bf16[512,128]{1,0:T(8,128)(2,1)S(1)}) custom-call(s32[4]{0:T(128)S(1)} %pad_add_fusion.c, bf16[512,2048]{1,0:T(8,128)(2,1)S(1)} %bitcast.115, bf16[2048,1024]{1,0:T(8,128)(2,1)S(1)} %copy-done, bf16[2048,1024]{1,0:T(8,128)(2,1)S(1)} %copy-done.3, ...), custom_call_target="tpu_custom_call" | custom-call | flops 3300000000 | bytes 10485760 | tf_op jit(solution)/shard_map/pallas_call | solution.py:34
  16.2 4.2 %shard_map.93 = (bf16[512,512]{1,0:T(8,128)(2,1)S(1)}, bf16[512,512]{1,0:T(8,128)(2,1)S(1)}, bf16[512,128]{1,0:T(8,128)(2,1)S(1)}, bf16[512,128]{1,0:T(8,128)(2,1)S(1)}) custom-call(s32[4]{0:T(128)S(1)} %pad_add_fusion.c, bf16[512,2048]{1,0:T(8,128)(2,1)S(1)} %collective-permute-done.t.tp, bf16[2048,1024]{1,0:T(8,128)(2,1)S(1)} %copy-done.4, ...), custom_call_target="tpu_custom_call" | custom-call | flops 2200000000 | bytes 7340032 | tf_op jit(solution)/shard_map/pallas_call | solution.py:34
  24.9 5.2 %shard_map.94 = (bf16[512,512]{1,0:T(8,128)(2,1)S(1)}, f32[1024,512]{1,0:T(8,128)S(1)}) custom-call(s32[4]{0:T(128)S(1)} %pad_add_fusion.c, bf16[512,2048]{1,0:T(8,128)(2,1)S(1)} %collective-permute-done.t.tp, bf16[2048,1024]{1,0:T(8,128)(2,1)S(1)} %copy-done.1, bf16[512,512]{1,0:T(8,128)(2,1)S(1)} %get-tuple-element.57.qo, ...), custom_call_target="tpu_custom_call" | custom-call | flops 2200000000 | bytes 10485760 | tf_op jit(solution)/shard_map/pallas_call | solution.py:34
  37.1 1.8 %collective-permute-start.7 = (bf16[512,512]{1,0:T(8,128)(2,1)}, bf16[512,512]{1,0:T(8,128)(2,1)}, u32[]{:S(2)}, u32[]{:S(2)}) collective-permute-start(bf16[512,512]{1,0:T(8,128)(2,1)} %slice_select_fusion), channel_id=1, source_target_pairs={{0,4},{4,0},{1,5},{5,1},{2,6},{6,2},{3,7},{7,3},{8,12},{12,8},{9,1... | collective-permute-start | bytes 1572872 | tf_op jit(solution)/shard_map/ppermute | solution.py:353
  40.4 2.3 %shard_map.95 = bf16[2048,1024]{1,0:T(8,128)(2,1)S(1)} custom-call(s32[4]{0:T(128)S(1)} %pad_add_fusion.c, bf16[512,2048]{1,0:T(8,128)(2,1)S(1)} %bitcast.116, bf16[512,2048]{1,0:T(8,128)(2,1)S(1)} %collective-permute-done.t.tp), custom_call_target="tpu_custom_call" | custom-call | flops 1000000 | bytes 8388608 | tf_op jit(solution)/shard_map/pallas_call | solution.py:34
  44.3 4.1 %shard_map.96 = (bf16[512,512]{1,0:T(8,128)(2,1)S(1)}, bf16[512,512]{1,0:T(8,128)(2,1)S(1)}, bf16[1024,512]{1,0:T(8,128)(2,1)S(1)}, bf16[512,128]{1,0:T(8,128)(2...) custom-call(s32[4]{0:T(128)S(1)} %pad_add_fusion.c, f32[1024,512]{1,0:T(8,128)S(1)} %copy-done.20, ...), custom_call_target="tpu_custom_call" | custom-call | flops 300000000 | bytes 7340032 | tf_op jit(solution)/shard_map/pallas_call | solution.py:34
  51.1 4.3 %shard_map.97.g.refs_0_ = bf16[1024,512]{1,0:T(8,128)(2,1)S(1)} custom-call(s32[4]{0:T(128)S(1)} %pad_add_fusion.c, bf16[512,512]{1,0:T(8,128)(2,1)S(1)} %get-tuple-element.58.ko, bf16[512,512]{1,0:T(8,128)(2,1)S(1)} %copy-done.12, bf16[512,512]{1,0:T(8,128)(2,1)S(1)} %get-tuple-element.59.vo, bf16[512,512]{1,0:T(8,128)(2,1)S(1)} %copy-done.14, ...), custom_call_target="tpu_custom_call" | custom-call | flops 1200000000 | bytes 4194304 | tf_op jit(solution)/shard_map/pallas_call | solution.py:34
  55.3 3.1 %shard_map.98 = bf16[4,4,4,32,512]{4,3,2,1,0:T(8,128)(2,1)S(1)} custom-call(s32[4]{0:T(128)S(1)} %pad_add_fusion.c, bf16[4,4,8,16,1024]{4,3,2,1,0:T(8,128)(2,1)S(1)} %bitcast.109, bf16[1024,512]{1,0:T(8,128)(2,1)S(1)} %shard_map.97.g.refs_0_), custom_call_target="tpu_custom_call" | custom-call | flops 2200000000 | bytes 9437184 | tf_op jit(solution)/shard_map/pallas_call | solution.py:34
  58.4 7.3 %shard_map.99 = (f32[1024,512]{1,0:T(8,128)S(1)}, f32[1024,512]{1,0:T(8,128)S(1)}) custom-call(s32[4]{0:T(128)S(1)} %pad_add_fusion.c, bf16[512,512]{1,0:T(8,128)(2,1)S(1)} %copy-done.18, bf16[512,512]{1,0:T(8,128)(2,1)S(1)} %copy-done.22, bf16[512,512]{1,0:T(8,128)(2,1)S(1)} %get-tuple-element.58.ko, bf16[512,512]{1,0:T(8,128)(2,1)S(1)} %copy-done.12, ...), custom_call_target="tpu_custom_call" | custom-call | flops 2000000000 | bytes 9437184 | tf_op jit(solution)/shard_map/pallas_call | solution.py:34
  66.3 2.3 %collective-permute-start.13 = (bf16[512,128]{1,0:T(8,128)(2,1)S(1)}, bf16[512,128]{1,0:T(8,128)(2,1)S(1)}, u32[]{:S(2)}, u32[]{:S(2)}) collective-permute-start(bf16[512,128]{1,0:T(8,128)(2,1)S(1)} %fusion.24), channel_id=1, source_target_pairs={{0,96},{32,0},{64,32},{96,64},{1,97},{33,1},{65,33},{97,65},{2,98}... | collective-permute-start | bytes 393224 | tf_op jit(solution)/shard_map/ppermute | solution.py:349
  70.5 2.2 %collective-permute-start.16 = (bf16[2,4,32,512]{3,2,1,0:T(8,128)(2,1)S(1)}, bf16[2,4,32,512]{3,2,1,0:T(8,128)(2,1)S(1)}, u32[]{:S(2)}, u32[]{:S(2)}) collective-permute-start(bf16[2,4,32,512]{3,2,1,0:T(8,128)(2,1)S(1)} %get-tuple-element.107), channel_id=1, source_target_pairs={{0,3},{1,0},{2,1},{3,2},{4,7},{5,4},{6,5},{7,6},{8,11},{9,8},{10,9... | collective-permute-start | bytes 786440 | tf_op jit(solution)/shard_map/ppermute | solution.py:349
  74.2 2.0 %shard_map.100 = (bf16[1024,512]{1,0:T(8,128)(2,1)S(1)}, bf16[1024,512]{1,0:T(8,128)(2,1)S(1)}) custom-call(s32[4]{0:T(128)S(1)} %pad_add_fusion.c, bf16[512,512]{1,0:T(8,128)(2,1)S(1)} %get-tuple-element.58.ko, bf16[512,512]{1,0:T(8,128)(2,1)S(1)} %copy-done.12, bf16[512,512]{1,0:T(8,128)(2,1)S(1)} %get-tuple-element.59.vo, ...), custom_call_target="tpu_custom_call" | custom-call | flops 200000000 | bytes 8388608 | tf_op jit(solution)/shard_map/pallas_call | solution.py:34
  78.7 2.7 %shard_map.103 = bf16[3,4,4,32,512]{4,3,2,1,0:T(8,128)(2,1)S(1)} custom-call(s32[4]{0:T(128)S(1)} %pad_add_fusion.c, bf16[4,4,8,16,1024]{4,3,2,1,0:T(8,128)(2,1)S(1)} %bitcast.112, bf16[1024,512]{1,0:T(8,128)(2,1)S(1)} %get-tuple-element.83.refs_2_.g), custom_call_target="tpu_custom_call" | custom-call | flops 1650000000 | bytes 7340032 | tf_op jit(solution)/shard_map/pallas_call | solution.py:34
  81.4 3.0 %shard_map.102 = bf16[3,4,4,32,512]{4,3,2,1,0:T(8,128)(2,1)S(1)} custom-call(s32[4]{0:T(128)S(1)} %pad_add_fusion.c, bf16[4,4,8,16,1024]{4,3,2,1,0:T(8,128)(2,1)S(1)} %bitcast.113, bf16[1024,512]{1,0:T(8,128)(2,1)S(1)} %get-tuple-element.82.refs_1_.g), custom_call_target="tpu_custom_call" | custom-call | flops 1650000000 | bytes 7340032 | tf_op jit(solution)/shard_map/pallas_call | solution.py:34
  87.7 3.4 %collective-permute-start.20 = (bf16[2,4,32,512]{3,2,1,0:T(8,128)(2,1)S(1)}, bf16[2,4,32,512]{3,2,1,0:T(8,128)(2,1)S(1)}, u32[]{:S(2)}, u32[]{:S(2)}) collective-permute-start(bf16[2,4,32,512]{3,2,1,0:T(8,128)(2,1)S(1)} %get-tuple-element.129), channel_id=1, source_target_pairs={{0,96},{32,0},{64,32},{96,64},{1,97},{33,1},{65,33},{97,65},{2,98}... | collective-permute-start | bytes 786440 | tf_op jit(solution)/shard_map/ppermute | solution.py:349
  91.3 3.8 %collective-permute-start.26 = (bf16[4,4,32,512]{3,2,1,0:T(8,128)(2,1)S(1)}, bf16[4,4,32,512]{3,2,1,0:T(8,128)(2,1)S(1)}, u32[]{:S(2)}, u32[]{:S(2)}) collective-permute-start(bf16[4,4,32,512]{3,2,1,0:T(8,128)(2,1)S(1)} %pad_maximum_fusion.5), channel_id=1, source_target_pairs={{0,3},{1,0},{2,1},{3,2},{4,7},{5,4},{6,5},{7,6},{8,11},{9,8},{10,9... | collective-permute-start | bytes 1572872 | tf_op jit(solution)/shard_map/ppermute | solution.py:349
  96.1 2.4 %collective-permute-start.24 = (bf16[4,4,32,512]{3,2,1,0:T(8,128)(2,1)S(1)}, bf16[4,4,32,512]{3,2,1,0:T(8,128)(2,1)S(1)}, u32[]{:S(2)}, u32[]{:S(2)}) collective-permute-start(bf16[4,4,32,512]{3,2,1,0:T(8,128)(2,1)S(1)} %pad_maximum_fusion.3), channel_id=1, source_target_pairs={{0,96},{32,0},{64,32},{96,64},{1,97},{33,1},{65,33},{97,65},{2,98}... | collective-permute-start | bytes 1572872 | tf_op jit(solution)/shard_map/ppermute | solution.py:349
  100.0 3.5 %collective-permute-done.26 = bf16[4,4,32,512]{3,2,1,0:T(8,128)(2,1)S(1)} collective-permute-done((bf16[4,4,32,512]{3,2,1,0:T(8,128)(2,1)S(1)}, bf16[4,4,32,512]{3,2,1,0:T(8,128)(2,1)S(1)}, u32[]{:S(2)}, u32[]{:S(2)}) %collective-permute-start.26) | collective-permute-done | bytes 524320 | tf_op jit(solution)/shard_map/ppermute | solution.py:349
  103.5 5.2 %shard_map.101 = bf16[512,2048]{1,0:T(8,128)(2,1)S(1)} custom-call(s32[4]{0:T(128)S(1)} %pad_add_fusion.c, bf16[1024,512]{1,0:T(8,128)(2,1)S(1)} %shard_map.97.g.refs_0_, bf16[1024,512]{1,0:T(8,128)(2,1)S(1)} %get-tuple-element.82.refs_1_.g, bf16[1024,512]{1,0:T(8,128)(2,1)S(1)} %get-tuple-element.83.refs_2_.g, bf16[2048,1024]{1,0:T(8,128)(2,1)S(1)} %copy-done.2, ...), custom_call_target="tpu_custom_call" | custom-call | flops 3300000000 | bytes 10485760 | tf_op jit(solution)/shard_map/pallas_call | solution.py:34
  109.6 4.8 %collective-permute-done.21 = bf16[4,4,32,512]{3,2,1,0:T(8,128)(2,1)S(1)} collective-permute-done((bf16[4,4,32,512]{3,2,1,0:T(8,128)(2,1)S(1)}, bf16[4,4,32,512]{3,2,1,0:T(8,128)(2,1)S(1)}, u32[]{:S(2)}, u32[]{:S(2)}) %collective-permute-start.21) | collective-permute-done | bytes 524320 | tf_op jit(solution)/shard_map/ppermute | solution.py:349
  114.3 4.7 %collective-permute-start.27 = (bf16[512,2048]{1,0:T(8,128)(2,1)S(1)}, bf16[512,2048]{1,0:T(8,128)(2,1)S(1)}, u32[]{:S(2)}, u32[]{:S(2)}) collective-permute-start(bf16[512,2048]{1,0:T(8,128)(2,1)S(1)} %shard_map.101), channel_id=1, source_target_pairs={{0,4},{4,0},{1,5},{5,1},{2,6},{6,2},{3,7},{7,3},{8,12},{12,8},{9,1... | collective-permute-start | bytes 6291464 | tf_op jit(solution)/shard_map/ppermute | solution.py:353
  119.4 2.7 %collective-permute-start.29 = (bf16[4,32,512]{2,1,0:T(8,128)(2,1)S(1)}, bf16[4,32,512]{2,1,0:T(8,128)(2,1)S(1)}, u32[]{:S(2)}, u32[]{:S(2)}) collective-permute-start(bf16[4,32,512]{2,1,0:T(8,128)(2,1)S(1)} %get-tuple-element.128), channel_id=1, source_target_pairs={{0,96},{32,0},{64,32},{96,64},{1,97},{33,1},{65,33},{97,65},{2,98}... | collective-permute-start | bytes 393224 | tf_op jit(solution)/shard_map/ppermute | solution.py:349
  123.6 2.1 %collective-permute-done.28 = bf16[4,32,512]{2,1,0:T(8,128)(2,1)S(1)} collective-permute-done((bf16[4,32,512]{2,1,0:T(8,128)(2,1)S(1)}, bf16[4,32,512]{2,1,0:T(8,128)(2,1)S(1)}, u32[]{:S(2)}, u32[]{:S(2)}) %collective-permute-start.28) | collective-permute-done | bytes 131104 | tf_op jit(solution)/shard_map/ppermute | solution.py:349
  130.0 7.4 %collective-permute-done.31 = bf16[2,4,32,512]{3,2,1,0:T(8,128)(2,1)S(1)} collective-permute-done((bf16[2,4,32,512]{3,2,1,0:T(8,128)(2,1)S(1)}, bf16[2,4,32,512]{3,2,1,0:T(8,128)(2,1)S(1)}, u32[]{:S(2)}, u32[]{:S(2)}) %collective-permute-start.31) | collective-permute-done | bytes 262176 | tf_op jit(solution)/shard_map/ppermute | solution.py:349
  137.6 6.1 %shard_map.106 = bf16[512,2048]{1,0:T(8,128)(2,1)} custom-call(s32[4]{0:T(128)S(1)} %pad_add_fusion.c, bf16[1024,512]{1,0:T(8,128)(2,1)S(1)} %shard_map.97.g.refs_0_, bf16[1024,512]{1,0:T(8,128)(2,1)S(1)} %get-tuple-element.82.refs_1_.g, bf16[1024,512]{1,0:T(8,128)(2,1)S(1)} %get-tuple-element.83.refs_2_.g, bf16[2048,1024]{1,0:T(8,128)(2,1)S(1)} %copy-done.2, ...), custom_call_target="tpu_custom_call" | custom-call | flops 3300000000 | bytes 10485760 | tf_op jit(solution)/shard_map/pallas_call | solution.py:34
  144.4 2.1 %collective-permute-start.35 = (bf16[32,512]{1,0:T(8,128)(2,1)S(1)}, bf16[32,512]{1,0:T(8,128)(2,1)S(1)}, u32[]{:S(2)}, u32[]{:S(2)}) collective-permute-start(bf16[32,512]{1,0:T(8,128)(2,1)S(1)} %get-tuple-element.135), channel_id=1, source_target_pairs={{0,96},{32,0},{64,32},{96,64},{1,97},{33,1},{65,33},{97,65},{2,98}... | collective-permute-start | bytes 98312 | tf_op jit(solution)/shard_map/ppermute | solution.py:349
  147.9 3.3 %collective-permute-start.38 = (bf16[32,1024]{1,0:T(8,128)(2,1)S(1)}, bf16[32,1024]{1,0:T(8,128)(2,1)S(1)}, u32[]{:S(2)}, u32[]{:S(2)}) collective-permute-start(bf16[32,1024]{1,0:T(8,128)(2,1)S(1)} %get-tuple-element.138), channel_id=1, source_target_pairs={{0,3},{1,0},{2,1},{3,2},{4,7},{5,4},{6,5},{7,6},{8,11},{9,8},{10,9... | collective-permute-start | bytes 196616 | tf_op jit(solution)/shard_map/ppermute | solution.py:349
  152.5 3.4 %collective-permute-done.39 = bf16[32,1024]{1,0:T(8,128)(2,1)S(1)} collective-permute-done((bf16[32,1024]{1,0:T(8,128)(2,1)S(1)}, bf16[32,1024]{1,0:T(8,128)(2,1)S(1)}, u32[]{:S(2)}, u32[]{:S(2)}) %collective-permute-start.39) | collective-permute-done | bytes 65568 | tf_op jit(solution)/shard_map/ppermute | solution.py:349
  156.0 4.3 %collective-permute-start.40 = (bf16[16,1536]{1,0:T(8,128)(2,1)S(1)}, bf16[16,1536]{1,0:T(8,128)(2,1)S(1)}, u32[]{:S(2)}, u32[]{:S(2)}) collective-permute-start(bf16[16,1536]{1,0:T(8,128)(2,1)S(1)} %broadcast_select_fusion.1), channel_id=1, source_target_pairs={{0,4},{4,0},{1,5},{5,1},{2,6},{6,2},{3,7},{7,3},{8,12},{12,8},{9,1... | collective-permute-start | bytes 147464 | tf_op jit(solution)/shard_map/ppermute | solution.py:353
  (159 shorter events, 46.1 us)
Async XLA Ops:
  0.6 15.6 %collective-permute-start = (bf16[512,2048]{1,0:T(8,128)(2,1)}, bf16[512,2048]{1,0:T(8,128)(2,1)S(1)}, u32[]{:S(2)}, u32[]{:S(2)}) collective-permute-start(bf16[512,2048]{1,0:T(8,128)(2,1)} %bitcast.114), channel_id=1, source_target_pairs={{0,4},{4,0},{1,5},{5,1},{2,6},{6,2},{3,7},{7,3},{8,12},{12,8},{9,1... | collective-permute-start | bytes 6291464 | tf_op jit(solution)/shard_map/ppermute | solution.py:353
  20.5 10.5 %collective-permute-start.1 = (bf16[512,128]{1,0:T(8,128)(2,1)S(1)}, bf16[512,128]{1,0:T(8,128)(2,1)S(1)}, u32[]{:S(2)}, u32[]{:S(2)}) collective-permute-start(bf16[512,128]{1,0:T(8,128)(2,1)S(1)} %get-tuple-element.56), channel_id=1, source_target_pairs={{0,8},{8,16},{16,24},{24,0},{1,9},{9,17},{17,25},{25,1},{2,10},{10... | collective-permute-start | bytes 393224 | tf_op jit(solution)/shard_map/ppermute | solution.py:349
  21.9 9.1 %collective-permute-start.2 = (bf16[512,128]{1,0:T(8,128)(2,1)S(1)}, bf16[512,128]{1,0:T(8,128)(2,1)S(1)}, u32[]{:S(2)}, u32[]{:S(2)}) collective-permute-start(bf16[512,128]{1,0:T(8,128)(2,1)S(1)} %get-tuple-element.56), channel_id=1, source_target_pairs={{0,24},{8,0},{16,8},{24,16},{1,25},{9,1},{17,9},{25,17},{2,26},{10... | collective-permute-start | bytes 393224 | tf_op jit(solution)/shard_map/ppermute | solution.py:349
  23.2 7.7 %collective-permute-start.3 = (bf16[512,128]{1,0:T(8,128)(2,1)S(1)}, bf16[512,128]{1,0:T(8,128)(2,1)S(1)}, u32[]{:S(2)}, u32[]{:S(2)}) collective-permute-start(bf16[512,128]{1,0:T(8,128)(2,1)S(1)} %get-tuple-element.56), channel_id=1, source_target_pairs={{0,16},{8,24},{16,0},{24,8},{1,17},{9,25},{17,1},{25,9},{2,18},{10... | collective-permute-start | bytes 393224 | tf_op jit(solution)/shard_map/ppermute | solution.py:349
  31.8 10.9 %collective-permute-start.4 = (bf16[512,128]{1,0:T(8,128)(2,1)}, bf16[512,128]{1,0:T(8,128)(2,1)}, u32[]{:S(2)}, u32[]{:S(2)}) collective-permute-start(bf16[512,128]{1,0:T(8,128)(2,1)} %fusion.20), channel_id=1, source_target_pairs={{0,32},{32,64},{64,96},{96,0},{1,33},{33,65},{65,97},{97,1},{2,34}... | collective-permute-start | bytes 393224 | tf_op jit(solution)/shard_map/ppermute | solution.py:349
  33.1 9.7 %collective-permute-start.5 = (bf16[512,128]{1,0:T(8,128)(2,1)}, bf16[512,128]{1,0:T(8,128)(2,1)}, u32[]{:S(2)}, u32[]{:S(2)}) collective-permute-start(bf16[512,128]{1,0:T(8,128)(2,1)} %fusion.20), channel_id=1, source_target_pairs={{0,96},{32,0},{64,32},{96,64},{1,97},{33,1},{65,33},{97,65},{2,98}... | collective-permute-start | bytes 393224 | tf_op jit(solution)/shard_map/ppermute | solution.py:349
  34.6 8.2 %collective-permute-start.6 = (bf16[512,128]{1,0:T(8,128)(2,1)}, bf16[512,128]{1,0:T(8,128)(2,1)}, u32[]{:S(2)}, u32[]{:S(2)}) collective-permute-start(bf16[512,128]{1,0:T(8,128)(2,1)} %fusion.20), channel_id=1, source_target_pairs={{0,64},{32,96},{64,0},{96,32},{1,65},{33,97},{65,1},{97,33},{2,66}... | collective-permute-start | bytes 393224 | tf_op jit(solution)/shard_map/ppermute | solution.py:349
  37.1 7.1 %collective-permute-start.7 = (bf16[512,512]{1,0:T(8,128)(2,1)}, bf16[512,512]{1,0:T(8,128)(2,1)}, u32[]{:S(2)}, u32[]{:S(2)}) collective-permute-start(bf16[512,512]{1,0:T(8,128)(2,1)} %slice_select_fusion), channel_id=1, source_target_pairs={{0,4},{4,0},{1,5},{5,1},{2,6},{6,2},{3,7},{7,3},{8,12},{12,8},{9,1... | collective-permute-start | bytes 1572872 | tf_op jit(solution)/shard_map/ppermute | solution.py:353
  48.4 17.4 %collective-permute-start.10 = (bf16[512,128]{1,0:T(8,128)(2,1)S(1)}, bf16[512,128]{1,0:T(8,128)(2,1)S(1)}, u32[]{:S(2)}, u32[]{:S(2)}) collective-permute-start(bf16[512,128]{1,0:T(8,128)(2,1)S(1)} %get-tuple-element.72), channel_id=1, source_target_pairs={{0,24},{8,0},{16,8},{24,16},{1,25},{9,1},{17,9},{25,17},{2,26},{10... | collective-permute-start | bytes 393224 | tf_op jit(solution)/shard_map/ppermute | solution.py:349
  49.9 15.9 %collective-permute-start.11 = (bf16[512,128]{1,0:T(8,128)(2,1)S(1)}, bf16[512,128]{1,0:T(8,128)(2,1)S(1)}, u32[]{:S(2)}, u32[]{:S(2)}) collective-permute-start(bf16[512,128]{1,0:T(8,128)(2,1)S(1)} %get-tuple-element.72), channel_id=1, source_target_pairs={{0,16},{8,24},{16,0},{24,8},{1,17},{9,25},{17,1},{25,9},{2,18},{10... | collective-permute-start | bytes 393224 | tf_op jit(solution)/shard_map/ppermute | solution.py:349
  51.1 14.7 %collective-permute-start.9 = (bf16[512,128]{1,0:T(8,128)(2,1)S(1)}, bf16[512,128]{1,0:T(8,128)(2,1)S(1)}, u32[]{:S(2)}, u32[]{:S(2)}) collective-permute-start(bf16[512,128]{1,0:T(8,128)(2,1)S(1)} %get-tuple-element.72), channel_id=1, source_target_pairs={{0,8},{8,16},{16,24},{24,0},{1,9},{9,17},{17,25},{25,1},{2,10},{10... | collective-permute-start | bytes 393224 | tf_op jit(solution)/shard_map/ppermute | solution.py:349
  65.9 6.8 %collective-permute-start.12 = (bf16[512,128]{1,0:T(8,128)(2,1)S(1)}, bf16[512,128]{1,0:T(8,128)(2,1)S(1)}, u32[]{:S(2)}, u32[]{:S(2)}) collective-permute-start(bf16[512,128]{1,0:T(8,128)(2,1)S(1)} %fusion.24), channel_id=1, source_target_pairs={{0,32},{32,64},{64,96},{96,0},{1,33},{33,65},{65,97},{97,1},{2,34}... | collective-permute-start | bytes 393224 | tf_op jit(solution)/shard_map/ppermute | solution.py:349
  66.3 7.6 %collective-permute-start.13 = (bf16[512,128]{1,0:T(8,128)(2,1)S(1)}, bf16[512,128]{1,0:T(8,128)(2,1)S(1)}, u32[]{:S(2)}, u32[]{:S(2)}) collective-permute-start(bf16[512,128]{1,0:T(8,128)(2,1)S(1)} %fusion.24), channel_id=1, source_target_pairs={{0,96},{32,0},{64,32},{96,64},{1,97},{33,1},{65,33},{97,65},{2,98}... | collective-permute-start | bytes 393224 | tf_op jit(solution)/shard_map/ppermute | solution.py:349
  68.8 15.7 %collective-permute-start.15 = (bf16[2,4,32,512]{3,2,1,0:T(8,128)(2,1)S(1)}, bf16[2,4,32,512]{3,2,1,0:T(8,128)(2,1)S(1)}, u32[]{:S(2)}, u32[]{:S(2)}) collective-permute-start(bf16[2,4,32,512]{3,2,1,0:T(8,128)(2,1)S(1)} %get-tuple-element.108), channel_id=1, source_target_pairs={{0,1},{1,2},{2,3},{3,0},{4,5},{5,6},{6,7},{7,4},{8,9},{9,10},{10,1... | collective-permute-start | bytes 786440 | tf_op jit(solution)/shard_map/ppermute | solution.py:349
  70.5 14.0 %collective-permute-start.16 = (bf16[2,4,32,512]{3,2,1,0:T(8,128)(2,1)S(1)}, bf16[2,4,32,512]{3,2,1,0:T(8,128)(2,1)S(1)}, u32[]{:S(2)}, u32[]{:S(2)}) collective-permute-start(bf16[2,4,32,512]{3,2,1,0:T(8,128)(2,1)S(1)} %get-tuple-element.107), channel_id=1, source_target_pairs={{0,3},{1,0},{2,1},{3,2},{4,7},{5,4},{6,5},{7,6},{8,11},{9,8},{10,9... | collective-permute-start | bytes 786440 | tf_op jit(solution)/shard_map/ppermute | solution.py:349
  84.5 10.6 %collective-permute-start.17 = (bf16[2,4,32,512]{3,2,1,0:T(8,128)(2,1)S(1)}, bf16[2,4,32,512]{3,2,1,0:T(8,128)(2,1)S(1)}, u32[]{:S(2)}, u32[]{:S(2)}) collective-permute-start(bf16[2,4,32,512]{3,2,1,0:T(8,128)(2,1)S(1)} %get-tuple-element.132), channel_id=1, source_target_pairs={{0,8},{8,16},{16,24},{24,0},{1,9},{9,17},{17,25},{25,1},{2,10},{10... | collective-permute-start | bytes 786440 | tf_op jit(solution)/shard_map/ppermute | solution.py:349
  86.2 9.3 %collective-permute-start.18 = (bf16[2,4,32,512]{3,2,1,0:T(8,128)(2,1)S(1)}, bf16[2,4,32,512]{3,2,1,0:T(8,128)(2,1)S(1)}, u32[]{:S(2)}, u32[]{:S(2)}) collective-permute-start(bf16[2,4,32,512]{3,2,1,0:T(8,128)(2,1)S(1)} %get-tuple-element.131), channel_id=1, source_target_pairs={{0,24},{8,0},{16,8},{24,16},{1,25},{9,1},{17,9},{25,17},{2,26},{10... | collective-permute-start | bytes 786440 | tf_op jit(solution)/shard_map/ppermute | solution.py:349
  87.5 7.9 %collective-permute-start.19 = (bf16[2,4,32,512]{3,2,1,0:T(8,128)(2,1)S(1)}, bf16[2,4,32,512]{3,2,1,0:T(8,128)(2,1)S(1)}, u32[]{:S(2)}, u32[]{:S(2)}) collective-permute-start(bf16[2,4,32,512]{3,2,1,0:T(8,128)(2,1)S(1)} %get-tuple-element.130), channel_id=1, source_target_pairs={{0,32},{32,64},{64,96},{96,0},{1,33},{33,65},{65,97},{97,1},{2,34}... | collective-permute-start | bytes 786440 | tf_op jit(solution)/shard_map/ppermute | solution.py:349
  87.7 7.8 %collective-permute-start.20 = (bf16[2,4,32,512]{3,2,1,0:T(8,128)(2,1)S(1)}, bf16[2,4,32,512]{3,2,1,0:T(8,128)(2,1)S(1)}, u32[]{:S(2)}, u32[]{:S(2)}) collective-permute-start(bf16[2,4,32,512]{3,2,1,0:T(8,128)(2,1)S(1)} %get-tuple-element.129), channel_id=1, source_target_pairs={{0,96},{32,0},{64,32},{96,64},{1,97},{33,1},{65,33},{97,65},{2,98}... | collective-permute-start | bytes 786440 | tf_op jit(solution)/shard_map/ppermute | solution.py:349
  91.3 12.2 %collective-permute-start.26 = (bf16[4,4,32,512]{3,2,1,0:T(8,128)(2,1)S(1)}, bf16[4,4,32,512]{3,2,1,0:T(8,128)(2,1)S(1)}, u32[]{:S(2)}, u32[]{:S(2)}) collective-permute-start(bf16[4,4,32,512]{3,2,1,0:T(8,128)(2,1)S(1)} %pad_maximum_fusion.5), channel_id=1, source_target_pairs={{0,3},{1,0},{2,1},{3,2},{4,7},{5,4},{6,5},{7,6},{8,11},{9,8},{10,9... | collective-permute-start | bytes 1572872 | tf_op jit(solution)/shard_map/ppermute | solution.py:349
  95.2 13.6 %collective-permute-start.25 = (bf16[4,4,32,512]{3,2,1,0:T(8,128)(2,1)S(1)}, bf16[4,4,32,512]{3,2,1,0:T(8,128)(2,1)S(1)}, u32[]{:S(2)}, u32[]{:S(2)}) collective-permute-start(bf16[4,4,32,512]{3,2,1,0:T(8,128)(2,1)S(1)} %pad_maximum_fusion.4), channel_id=1, source_target_pairs={{0,1},{1,2},{2,3},{3,0},{4,5},{5,6},{6,7},{7,4},{8,9},{9,10},{10,1... | collective-permute-start | bytes 1572872 | tf_op jit(solution)/shard_map/ppermute | solution.py:349
  96.1 12.6 %collective-permute-start.24 = (bf16[4,4,32,512]{3,2,1,0:T(8,128)(2,1)S(1)}, bf16[4,4,32,512]{3,2,1,0:T(8,128)(2,1)S(1)}, u32[]{:S(2)}, u32[]{:S(2)}) collective-permute-start(bf16[4,4,32,512]{3,2,1,0:T(8,128)(2,1)S(1)} %pad_maximum_fusion.3), channel_id=1, source_target_pairs={{0,96},{32,0},{64,32},{96,64},{1,97},{33,1},{65,33},{97,65},{2,98}... | collective-permute-start | bytes 1572872 | tf_op jit(solution)/shard_map/ppermute | solution.py:349
  98.5 11.0 %collective-permute-start.23 = (bf16[4,4,32,512]{3,2,1,0:T(8,128)(2,1)S(1)}, bf16[4,4,32,512]{3,2,1,0:T(8,128)(2,1)S(1)}, u32[]{:S(2)}, u32[]{:S(2)}) collective-permute-start(bf16[4,4,32,512]{3,2,1,0:T(8,128)(2,1)S(1)} %pad_maximum_fusion.2), channel_id=1, source_target_pairs={{0,32},{32,64},{64,96},{96,0},{1,33},{33,65},{65,97},{97,1},{2,34}... | collective-permute-start | bytes 1572872 | tf_op jit(solution)/shard_map/ppermute | solution.py:349
  98.7 10.9 %collective-permute-start.22 = (bf16[4,4,32,512]{3,2,1,0:T(8,128)(2,1)S(1)}, bf16[4,4,32,512]{3,2,1,0:T(8,128)(2,1)S(1)}, u32[]{:S(2)}, u32[]{:S(2)}) collective-permute-start(bf16[4,4,32,512]{3,2,1,0:T(8,128)(2,1)S(1)} %pad_maximum_fusion.1), channel_id=1, source_target_pairs={{0,24},{8,0},{16,8},{24,16},{1,25},{9,1},{17,9},{25,17},{2,26},{10... | collective-permute-start | bytes 1572872 | tf_op jit(solution)/shard_map/ppermute | solution.py:349
  103.5 10.9 %collective-permute-start.21 = (bf16[4,4,32,512]{3,2,1,0:T(8,128)(2,1)S(1)}, bf16[4,4,32,512]{3,2,1,0:T(8,128)(2,1)S(1)}, u32[]{:S(2)}, u32[]{:S(2)}) collective-permute-start(bf16[4,4,32,512]{3,2,1,0:T(8,128)(2,1)S(1)} %pad_maximum_fusion), channel_id=1, source_target_pairs={{0,8},{8,16},{16,24},{24,0},{1,9},{9,17},{17,25},{25,1},{2,10},{10... | collective-permute-start | bytes 1572872 | tf_op jit(solution)/shard_map/ppermute | solution.py:349
  114.3 23.2 %collective-permute-start.27 = (bf16[512,2048]{1,0:T(8,128)(2,1)S(1)}, bf16[512,2048]{1,0:T(8,128)(2,1)S(1)}, u32[]{:S(2)}, u32[]{:S(2)}) collective-permute-start(bf16[512,2048]{1,0:T(8,128)(2,1)S(1)} %shard_map.101), channel_id=1, source_target_pairs={{0,4},{4,0},{1,5},{5,1},{2,6},{6,2},{3,7},{7,3},{8,12},{12,8},{9,1... | collective-permute-start | bytes 6291464 | tf_op jit(solution)/shard_map/ppermute | solution.py:353
  119.4 7.9 %collective-permute-start.29 = (bf16[4,32,512]{2,1,0:T(8,128)(2,1)S(1)}, bf16[4,32,512]{2,1,0:T(8,128)(2,1)S(1)}, u32[]{:S(2)}, u32[]{:S(2)}) collective-permute-start(bf16[4,32,512]{2,1,0:T(8,128)(2,1)S(1)} %get-tuple-element.128), channel_id=1, source_target_pairs={{0,96},{32,0},{64,32},{96,64},{1,97},{33,1},{65,33},{97,65},{2,98}... | collective-permute-start | bytes 393224 | tf_op jit(solution)/shard_map/ppermute | solution.py:349
  123.5 13.9 %collective-permute-start.31 = (bf16[2,4,32,512]{3,2,1,0:T(8,128)(2,1)S(1)}, bf16[2,4,32,512]{3,2,1,0:T(8,128)(2,1)S(1)}, u32[]{:S(2)}, u32[]{:S(2)}) collective-permute-start(bf16[2,4,32,512]{3,2,1,0:T(8,128)(2,1)S(1)} %get-tuple-element.119), channel_id=1, source_target_pairs={{0,8},{8,16},{16,24},{24,0},{1,9},{9,17},{17,25},{25,1},{2,10},{10... | collective-permute-start | bytes 786440 | tf_op jit(solution)/shard_map/ppermute | solution.py:349
  125.7 11.7 %collective-permute-start.32 = (bf16[2,4,32,512]{3,2,1,0:T(8,128)(2,1)S(1)}, bf16[2,4,32,512]{3,2,1,0:T(8,128)(2,1)S(1)}, u32[]{:S(2)}, u32[]{:S(2)}) collective-permute-start(bf16[2,4,32,512]{3,2,1,0:T(8,128)(2,1)S(1)} %get-tuple-element.121), channel_id=1, source_target_pairs={{0,24},{8,0},{16,8},{24,16},{1,25},{9,1},{17,9},{25,17},{2,26},{10... | collective-permute-start | bytes 786440 | tf_op jit(solution)/shard_map/ppermute | solution.py:349
  127.3 10.1 %collective-permute-start.33 = (bf16[2,4,32,512]{3,2,1,0:T(8,128)(2,1)S(1)}, bf16[2,4,32,512]{3,2,1,0:T(8,128)(2,1)S(1)}, u32[]{:S(2)}, u32[]{:S(2)}) collective-permute-start(bf16[2,4,32,512]{3,2,1,0:T(8,128)(2,1)S(1)} %get-tuple-element.120), channel_id=1, source_target_pairs={{0,16},{8,24},{16,0},{24,8},{1,17},{9,25},{17,1},{25,9},{2,18},{10... | collective-permute-start | bytes 786440 | tf_op jit(solution)/shard_map/ppermute | solution.py:349
  128.8 31.5 %collective-permute-start.8 = (bf16[512,512]{1,0:T(8,128)(2,1)S(1)}, bf16[512,512]{1,0:T(8,128)(2,1)S(1)}, u32[]{:S(2)}, u32[]{:S(2)}) collective-permute-start(bf16[512,512]{1,0:T(8,128)(2,1)S(1)} %get-tuple-element.69), channel_id=1, source_target_pairs={{0,4},{4,0},{1,5},{5,1},{2,6},{6,2},{3,7},{7,3},{8,12},{12,8},{9,1... | collective-permute-start | bytes 1572872 | tf_op jit(solution)/shard_map/ppermute | solution.py:353
  144.4 6.8 %collective-permute-start.35 = (bf16[32,512]{1,0:T(8,128)(2,1)S(1)}, bf16[32,512]{1,0:T(8,128)(2,1)S(1)}, u32[]{:S(2)}, u32[]{:S(2)}) collective-permute-start(bf16[32,512]{1,0:T(8,128)(2,1)S(1)} %get-tuple-element.135), channel_id=1, source_target_pairs={{0,96},{32,0},{64,32},{96,64},{1,97},{33,1},{65,33},{97,65},{2,98}... | collective-permute-start | bytes 98312 | tf_op jit(solution)/shard_map/ppermute | solution.py:349
  (36 other events, 196.1 us)
